TPU v7x, 32 devices: a whole 2x2x4 slice. The times are simulated.
32 devices in a mesh: narrow: 8 (over z, y), wide: 4 (over x, core).
Axes of the slice: x: 2, y: 2, z: 4, core: 2. Of those that a mesh axis runs over, the one named last changes fastest.
Arguments:
- frame_tokens: bfloat16 [96, 197, 768], P('narrow', None, 'wide'), may hold values from -6 to 6
- cotangent: bfloat16 [96, 197, 768], P('narrow', None, 'wide'), may hold values from -6 to 6
- caption_count: int32 [12], replicated, may hold values from 1 to 5, as said below
- caption_len: int32 [12, 5], replicated, may hold values from 1 to 77, as said below
- message_weight: bfloat16 [768, 768], replicated, may hold values from -0.21875 to 0.21875
- message_bias: float32 [768], replicated, may hold values from -3 to 3
- message_gain: float32 [768], replicated, may hold values from 0.5 to 1.5
- message_shift: float32 [768], replicated, may hold values from -2 to 2
- cross_qkv: bfloat16 [768, 3, 768], P(None, None, 'wide'), may hold values from -0.21875 to 0.21875
- cross_bias: float32 [2, 768], P(None, 'wide'), may hold values from -3 to 3
- cross_proj: bfloat16 [768, 768], P('wide'), may hold values from -0.4375 to 0.4375
- cross_offset: float32 [768], replicated, may hold values from -2 to 2
- attn_gain: float32 [768], replicated, may hold values from 0.5 to 1.5
- attn_shift: float32 [768], replicated, may hold values from -2 to 2
- qkv_weight: bfloat16 [768, 3, 768], P(None, None, 'wide'), may hold values from -0.21875 to 0.21875
- qkv_bias: float32 [2, 768], P(None, 'wide'), may hold values from -3 to 3
- out_weight: bfloat16 [768, 768], P('wide'), may hold values from -1.25 to 1.25
- out_bias: float32 [768], P('wide'), may hold values from -2 to 2
- mlp_gain: float32 [768], replicated, may hold values from 0.5 to 1.5
- mlp_shift: float32 [768], replicated, may hold values from -2 to 2
- up_weight: bfloat16 [768, 3072], P(None, 'wide'), may hold values from -0.21650635 to 0.21650635
- up_bias: float32 [3072], P('wide'), may hold values from -3 to 3
- down_weight: bfloat16 [3072, 768], P('wide'), may hold values from -0.109375 to 0.109375
- down_bias: float32 [768], P('wide'), may hold values from -2 to 2
Outputs:
- output_tokens: bfloat16 [96, 197, 768], P('narrow', None, 'wide')
- grad_tokens: bfloat16 [96, 197, 768], P('narrow', None, 'wide')
- grad_message_weight: float32 [768, 768], replicated
- grad_message_bias: float32 [768], replicated
- grad_message_gain: float32 [768], replicated
- grad_message_shift: float32 [768], replicated
- grad_cross_qkv: float32 [768, 3, 768], P(None, None, 'wide')
- grad_cross_bias: float32 [2, 768], P(None, 'wide')
- grad_cross_proj: float32 [768, 768], P('wide')
- grad_cross_offset: float32 [768], replicated
- grad_attn_gain: float32 [768], replicated
- grad_attn_shift: float32 [768], replicated
- grad_qkv_weight: float32 [768, 3, 768], P(None, None, 'wide')
- grad_qkv_bias: float32 [2, 768], P(None, 'wide')
- grad_out_weight: float32 [768, 768], P('wide')
- grad_out_bias: float32 [768], P('wide')
- grad_mlp_gain: float32 [768], replicated
- grad_mlp_shift: float32 [768], replicated
- grad_up_weight: float32 [768, 3072], P(None, 'wide')
- grad_up_bias: float32 [3072], P('wide')
- grad_down_weight: float32 [3072, 768], P('wide')
- grad_down_bias: float32 [768], P('wide')
Inputs may be any that keep to these rules, and one draw needn't show every extreme that they name: Captions of each video; a video uses its first caption_count slots. `caption_len`: words of a caption slot; slots at or after a video's caption_count are unused and hold a value too.
All inputs are finite; a program needn't handle non-finite values.
Results may differ from a plain program's by a relative error of at most 0.02.
Values may be sent and summed in bfloat16 or wider, within the bound.
No kernel may reach another device: no remote copies, remote signals or barrier semaphores. Data moves between devices by JAX's collectives and lax.ppermute only.
A program may use at most 192 MiB of HBM per device.

v0:
```python
import jax
import jax.numpy as jnp
from jax import lax
from jax.sharding import PartitionSpec as P

VIDEO_FRAMES = 8
HD = 64


eps_norm = 1e-05


def from_behind(block, axis, distance):
    devices = range(lax.axis_size(axis))
    route = [(i - distance, i) for i in devices if i - distance in devices]
    return lax.ppermute(block, axis, route)


def mat_mul(left, right):
    return jnp.dot(left, right, preferred_element_type=jnp.float32)


def mat_tn(left, right):
    return lax.dot_general(
        left, right, (((0,), (0,)), ((), ())), preferred_element_type=jnp.float32
    )


def mat_nt(left, right):
    return lax.dot_general(
        left, right, (((1,), (1,)), ((), ())), preferred_element_type=jnp.float32
    )


def normalize(values):
    row_mean = jnp.mean(values, axis=-1, keepdims=True)
    centred = values - row_mean
    inv_std = lax.rsqrt(jnp.mean(centred * centred, axis=-1, keepdims=True) + eps_norm)
    return (centred * inv_std, inv_std)


def norm_back(grad_norm, normed, inv_std, norm_gain):
    scaled = grad_norm * norm_gain
    return inv_std * (
        scaled
        - jnp.mean(scaled, axis=-1, keepdims=True)
        - normed * jnp.mean(scaled * normed, axis=-1, keepdims=True)
    )


def fetch_near(key_pair, offset):
    return from_behind(key_pair, "narrow", offset)


def return_near(grad_block, offset):
    return from_behind(grad_block, "narrow", offset)


def body(
    frame_tokens,
    cotangent,
    caption_count,
    caption_len,
    message_weight,
    message_bias,
    message_gain,
    message_shift,
    cross_qkv,
    cross_bias,
    cross_proj,
    cross_offset,
    attn_gain,
    attn_shift,
    qkv_weight,
    qkv_bias,
    out_weight,
    out_bias,
    mlp_gain,
    mlp_shift,
    up_weight,
    up_bias,
    down_weight,
    down_bias,
):
    frames, patches, width_part = frame_tokens.shape
    seq_len = patches + 1
    model_width = message_weight.shape[0]
    local_heads = width_part // HD
    row_count = frames * seq_len
    score_scale = HD ** (-0.5)
    low_type = jnp.bfloat16
    highest = lax.Precision.HIGHEST
    col_start = lax.axis_index("wide") * width_part
    narrow_idx = lax.axis_index("narrow")
    full_tokens = lax.all_gather(frame_tokens, "wide", axis=2, tiled=True)
    cls_rows = full_tokens[:, 0, :]
    message = mat_mul(cls_rows, message_weight) + message_bias
    msg_normed, msg_inv = normalize(message)
    msg_in = (msg_normed * message_gain + message_shift).astype(low_type)
    cross_flat = cross_qkv.reshape(model_width, 3 * width_part)
    cross_all = mat_mul(msg_in, cross_flat).reshape(frames, 3, width_part)
    cross_query = (cross_all[:, 0] + cross_bias[0]).astype(low_type)
    cross_key = cross_all[:, 1].astype(low_type)
    cross_value = (cross_all[:, 2] + cross_bias[1]).astype(low_type)
    key_pair = jnp.stack([cross_key, cross_value])
    near_reach = (frames + VIDEO_FRAMES - 2) // frames
    offsets = list(range(near_reach, 0, -1)) + [0] + list(range(-1, -near_reach - 1, -1))
    fetched = {0: key_pair}
    for offset in offsets:
        if offset != 0:
            fetched[offset] = fetch_near(key_pair, offset)
    window = jnp.concatenate([fetched[offset] for offset in offsets], axis=1)
    win_count = window.shape[1]
    win_frame = (narrow_idx - near_reach) * frames + jnp.arange(win_count)
    own_frame = narrow_idx * frames + jnp.arange(frames)
    same_video = own_frame[:, None] // VIDEO_FRAMES == win_frame[None, :] // VIDEO_FRAMES
    query_heads = cross_query.astype(jnp.float32).reshape(frames, local_heads, HD)
    key_heads = window[0].astype(jnp.float32).reshape(win_count, local_heads, HD)
    value_heads = window[1].astype(jnp.float32).reshape(win_count, local_heads, HD)
    cross_score = (
        jnp.einsum("thd,uhd->htu", query_heads, key_heads, precision=highest) * score_scale
    )
    cross_prob = jax.nn.softmax(jnp.where(same_video[None], cross_score, -1e30), axis=-1)
    cross_mix = jnp.einsum("htu,uhd->thd", cross_prob, value_heads, precision=highest)
    cross_mix = cross_mix.reshape(frames, width_part).astype(low_type)
    cross_sum = lax.psum(mat_mul(cross_mix, cross_proj), "wide")
    message_two = message + cross_sum + cross_offset
    full_cat = jnp.concatenate([full_tokens.astype(jnp.float32), message_two[:, None, :]], axis=1)
    attn_normed, attn_inv = normalize(full_cat)
    attn_in = (
        (attn_normed * attn_gain + attn_shift).astype(low_type).reshape(row_count, model_width)
    )
    qkv_flat = qkv_weight.reshape(model_width, 3 * width_part)
    proj_all = mat_mul(attn_in, qkv_flat).reshape(frames, seq_len, 3, width_part)
    queries = (
        (proj_all[:, :, 0] + qkv_bias[0]).astype(low_type).reshape(frames, seq_len, local_heads, HD)
    )
    key_rows = proj_all[:, :, 1].astype(low_type).reshape(frames, seq_len, local_heads, HD)
    value_rows = (
        (proj_all[:, :, 2] + qkv_bias[1]).astype(low_type).reshape(frames, seq_len, local_heads, HD)
    )
    scores = (
        jnp.einsum("tshd,tuhd->thsu", queries, key_rows, preferred_element_type=jnp.float32)
        * score_scale
    )
    score_top = jnp.max(scores, axis=-1, keepdims=True)
    exp_score = jnp.exp(scores - score_top)
    exp_sum = jnp.sum(exp_score, axis=-1, keepdims=True)
    log_total = score_top + jnp.log(exp_sum)
    attn_mix = jnp.einsum(
        "thsu,tuhd->tshd",
        (exp_score / exp_sum).astype(low_type),
        value_rows,
        preferred_element_type=jnp.float32,
    )
    attn_mix = attn_mix.astype(low_type).reshape(row_count, width_part)
    attn_branch = lax.psum_scatter(
        mat_mul(attn_mix, out_weight).reshape(frames, seq_len, model_width),
        "wide",
        scatter_dimension=2,
        tiled=True,
    )
    own_cat = lax.dynamic_slice_in_dim(full_cat, col_start, width_part, 2)
    hidden_res = own_cat + attn_branch + out_bias
    mixed_full = lax.all_gather(hidden_res.astype(low_type), "wide", axis=2, tiled=True)
    mlp_normed, mlp_inv = normalize(mixed_full.astype(jnp.float32))
    mlp_in = (mlp_normed * mlp_gain + mlp_shift).astype(low_type).reshape(row_count, model_width)
    pre_act = mat_mul(mlp_in, up_weight) + up_bias
    gate_sig = jax.nn.sigmoid(1.702 * pre_act)
    activated = (pre_act * gate_sig).astype(low_type)
    mlp_branch = lax.psum_scatter(
        mat_mul(activated, down_weight).reshape(frames, seq_len, model_width).astype(jnp.bfloat16),
        "wide",
        scatter_dimension=2,
        tiled=True,
    ).astype(jnp.float32)
    result = hidden_res + mlp_branch + down_bias
    output_tokens = result[:, :patches].astype(low_type)
    caption_slot = jnp.arange(caption_len.shape[1])
    word_total = jnp.sum(
        jnp.where(caption_slot[None, :] < caption_count[:, None], caption_len, 0), axis=1
    )
    word_total = word_total.astype(jnp.float32)
    video_scale = word_total / jnp.mean(word_total)
    own_video = own_frame // VIDEO_FRAMES
    video_match = own_video[:, None] == jnp.arange(video_scale.shape[0])[None, :]
    frame_weight = jnp.sum(jnp.where(video_match, video_scale[None, :], 0.0), axis=1)
    grad_res = jnp.concatenate(
        [
            cotangent.astype(jnp.float32) * frame_weight[:, None, None],
            jnp.zeros((frames, 1, width_part), jnp.float32),
        ],
        axis=1,
    )
    grad_down_bias = jnp.sum(grad_res, axis=(0, 1))
    grad_rows = lax.all_gather(grad_res.astype(low_type), "wide", axis=2, tiled=True).reshape(
        row_count, model_width
    )
    grad_down_weight = mat_tn(activated, grad_rows)
    grad_act = mat_nt(grad_rows, down_weight)
    grad_pre = (grad_act * (gate_sig + 1.702 * pre_act * gate_sig * (1.0 - gate_sig))).astype(
        low_type
    )
    grad_up_bias = jnp.sum(grad_pre, axis=0, dtype=jnp.float32)
    grad_up_weight = mat_tn(mlp_in, grad_pre)
    norm_term = mat_nt(grad_pre, up_weight).reshape(frames, seq_len, model_width)
    grad_mlp_in = lax.psum(norm_term, "wide")
    grad_mlp_gain = jnp.sum(grad_mlp_in * mlp_normed, axis=(0, 1))
    grad_mlp_shift = jnp.sum(grad_mlp_in, axis=(0, 1))
    grad_mixed = norm_back(grad_mlp_in, mlp_normed, mlp_inv, mlp_gain)
    grad_hidden = grad_res + lax.dynamic_slice_in_dim(grad_mixed, col_start, width_part, 2)
    grad_out_bias = jnp.sum(grad_hidden, axis=(0, 1))
    grad_full = lax.all_gather(grad_hidden.astype(low_type), "wide", axis=2, tiled=True).reshape(
        row_count, model_width
    )
    grad_out_weight = mat_tn(attn_mix, grad_full)
    grad_mix = (
        mat_nt(grad_full, out_weight).astype(low_type).reshape(frames, seq_len, local_heads, HD)
    )
    prob_again = jnp.exp(
        jnp.einsum("tshd,tuhd->thsu", queries, key_rows, preferred_element_type=jnp.float32)
        * score_scale
        - log_total
    )
    grad_value = jnp.einsum(
        "thsu,tshd->tuhd", prob_again.astype(low_type), grad_mix, preferred_element_type=jnp.float32
    )
    grad_prob = jnp.einsum(
        "tshd,tuhd->thsu", grad_mix, value_rows, preferred_element_type=jnp.float32
    )
    grad_score = (
        prob_again * (grad_prob - jnp.sum(prob_again * grad_prob, axis=-1, keepdims=True))
    ).astype(low_type)
    grad_query = (
        jnp.einsum("thsu,tuhd->tshd", grad_score, key_rows, preferred_element_type=jnp.float32)
        * score_scale
    )
    grad_key = (
        jnp.einsum("thsu,tshd->tuhd", grad_score, queries, preferred_element_type=jnp.float32)
        * score_scale
    )
    grad_proj = (
        jnp.stack([grad_query, grad_key, grad_value], axis=2)
        .astype(low_type)
        .reshape(row_count, 3 * width_part)
    )
    proj_sums = jnp.sum(grad_proj.reshape(row_count, 3, width_part), axis=0, dtype=jnp.float32)
    grad_qkv_bias = jnp.stack([proj_sums[0], proj_sums[2]])
    grad_qkv_weight = mat_tn(attn_in, grad_proj).reshape(model_width, 3, width_part)
    message_rest = lax.dynamic_update_slice_in_dim(
        jnp.zeros((frames, model_width), jnp.float32), grad_hidden[:, patches], col_start, 1
    )
    grad_attn_in, message_resid = lax.psum(
        (mat_nt(grad_proj, qkv_flat).reshape(frames, seq_len, model_width), message_rest), "wide"
    )
    grad_attn_gain = jnp.sum(grad_attn_in * attn_normed, axis=(0, 1))
    grad_attn_shift = jnp.sum(grad_attn_in, axis=(0, 1))
    grad_cat = norm_back(grad_attn_in, attn_normed, attn_inv, attn_gain)
    grad_message_two = grad_cat[:, patches] + message_resid
    grad_cross = grad_message_two.astype(low_type)
    grad_cross_offset = jnp.sum(grad_cross, axis=0, dtype=jnp.float32)
    grad_cross_proj = mat_tn(cross_mix, grad_cross)
    grad_cross_mix = mat_nt(grad_cross, cross_proj).astype(low_type).astype(jnp.float32)
    grad_cross_mix = grad_cross_mix.reshape(frames, local_heads, HD)
    grad_cross_prob = jnp.einsum("thd,uhd->htu", grad_cross_mix, value_heads, precision=highest)
    grad_cross_score = cross_prob * (
        grad_cross_prob - jnp.sum(cross_prob * grad_cross_prob, axis=-1, keepdims=True)
    )
    grad_cross_query = (
        jnp.einsum("htu,uhd->thd", grad_cross_score, key_heads, precision=highest) * score_scale
    )
    grad_win_key = (
        jnp.einsum("htu,thd->uhd", grad_cross_score, query_heads, precision=highest) * score_scale
    )
    grad_win_value = jnp.einsum("htu,thd->uhd", cross_prob, grad_cross_mix, precision=highest)
    grad_window = jnp.stack(
        [grad_win_key.reshape(win_count, width_part), grad_win_value.reshape(win_count, width_part)]
    )
    grad_blocks = {
        offset: grad_window[:, position * frames : (position + 1) * frames]
        for position, offset in enumerate(offsets)
    }
    grad_pair = grad_blocks[0]
    for offset in offsets:
        if offset != 0:
            grad_pair = grad_pair + return_near(grad_blocks[offset], -offset)
    grad_cross_all = jnp.stack(
        [grad_cross_query.reshape(frames, width_part), grad_pair[0], grad_pair[1]], axis=1
    )
    grad_cross_all = grad_cross_all.astype(low_type).reshape(frames, 3 * width_part)
    cross_sums = jnp.sum(grad_cross_all.reshape(frames, 3, width_part), axis=0, dtype=jnp.float32)
    grad_cross_bias = jnp.stack([cross_sums[0], cross_sums[2]])
    grad_cross_qkv = mat_tn(msg_in, grad_cross_all).reshape(model_width, 3, width_part)
    grad_msg_in = lax.psum(mat_nt(grad_cross_all, cross_flat), "wide")
    grad_message_gain = jnp.sum(grad_msg_in * msg_normed, axis=0)
    grad_message_shift = jnp.sum(grad_msg_in, axis=0)
    grad_message = (
        grad_message_two + norm_back(grad_msg_in, msg_normed, msg_inv, message_gain)
    ).astype(low_type)
    grad_message_bias = jnp.sum(grad_message, axis=0, dtype=jnp.float32)
    grad_message_weight = mat_tn(cls_rows, grad_message)
    grad_cls = lax.dynamic_slice_in_dim(
        mat_nt(grad_message, message_weight), col_start, width_part, 1
    )
    grad_patch = grad_hidden[:, :patches] + lax.dynamic_slice_in_dim(
        grad_cat[:, :patches], col_start, width_part, 2
    )
    grad_tokens = grad_patch.at[:, 0].add(grad_cls).astype(low_type)
    summed = lax.psum(
        (
            grad_message_weight,
            grad_message_bias,
            grad_message_gain,
            grad_message_shift,
            grad_cross_qkv,
            grad_cross_bias,
            grad_cross_proj,
            grad_cross_offset,
            grad_attn_gain,
            grad_attn_shift,
            grad_qkv_weight,
            grad_qkv_bias,
            grad_out_weight,
            grad_out_bias,
            grad_mlp_gain,
            grad_mlp_shift,
            grad_up_weight,
            grad_up_bias,
            grad_down_weight,
            grad_down_bias,
        ),
        "narrow",
    )
    return (output_tokens, grad_tokens) + tuple(summed)


def solution(mesh):
    return jax.shard_map(
        body,
        mesh=mesh,
        in_specs=(
            P("narrow", None, "wide"),
            P("narrow", None, "wide"),
            P(),
            P(),
            P(),
            P(),
            P(),
            P(),
            P(None, None, "wide"),
            P(None, "wide"),
            P("wide", None),
            P(),
            P(),
            P(),
            P(None, None, "wide"),
            P(None, "wide"),
            P("wide", None),
            P("wide"),
            P(),
            P(),
            P(None, "wide"),
            P("wide"),
            P("wide", None),
            P("wide"),
        ),
        out_specs=(
            P("narrow", None, "wide"),
            P("narrow", None, "wide"),
            P(),
            P(),
            P(),
            P(),
            P(None, None, "wide"),
            P(None, "wide"),
            P("wide", None),
            P(),
            P(),
            P(),
            P(None, None, "wide"),
            P(None, "wide"),
            P("wide", None),
            P("wide"),
            P(),
            P(),
            P(None, "wide"),
            P("wide"),
            P("wide", None),
            P("wide"),
        ),
        check_vma=False,
    )
```

profile of v0, /device:TPU:0, one launch (start us, length us, event | category | flops | bytes accessed | tf_op | source)
XLA Modules:
  0.0 1255.1 jit_solution(3297571914003000552)
XLA Ops:
  11.3 38.5 %all-gather.5.cloned.1.call-done = bf16[12,197,768]{1,2,0:T(8,128)(2,1)} async-done(((bf16[12,197,192]{1,2,0:T(8,128)(2,1)}), bf16[12,197,768]{1,2,0:T(8,128)(2,1)}) %all-gather.5.cloned.1.call-update) | async-done | bytes 3631120 | tf_op jit(solution)/shard_map/all_gather | solution.py:95
  58.8 4.5 collective-permute-start
  64.1 6.4 copy.353
  70.5 5.6 convert_element_type.186
  77.7 10.6 psum.175
  88.4 3.8 fusion.31
  97.0 2.9 fusion.7
  110.0 10.5 copy.361
  120.6 4.5 copy.372
  126.7 2.8 broadcast_multiply_fusion.1
  132.9 4.4 copy.373
  137.4 83.3 %reduce-scatter.3.cloned.1.call-done = f32[12,198,192]{1,0,2:T(8,128)} async-done(((f32[12,198,768]{1,0,2:T(8,128)}), f32[12,198,192]{1,0,2:T(8,128)}) %reduce-scatter.3.cloned.1.call-update) | async-done | bytes 1824784 | tf_op jit(solution)/shard_map/reduce_scatter | solution.py:157
  220.7 3.6 copy.362
  224.3 5.7 fusion.71
  232.6 27.8 %all-gather.9.cloned.1.call-done = bf16[12,198,768]{1,2,0:T(8,128)(2,1)} async-done(((bf16[12,198,192]{1,2,0:T(8,128)(2,1)}), bf16[12,198,768]{1,2,0:T(8,128)(2,1)}) %all-gather.9.cloned.1.call-update) | async-done | bytes 3649552 | tf_op jit(solution)/shard_map/all_gather | solution.py:196
  260.4 6.3 copy.374
  266.7 5.3 reshape.551
  272.0 27.9 %all-gather.7.cloned.1.call-done = bf16[12,198,768]{1,2,0:T(8,128)(2,1)} async-done(((bf16[12,198,192]{1,2,0:T(8,128)(2,1)}), bf16[12,198,768]{1,2,0:T(8,128)(2,1)}) %all-gather.7.cloned.1.call-update) | async-done | bytes 3649552 | tf_op jit(solution)/shard_map/all_gather | solution.py:165
  299.9 8.4 copy.364
  308.2 3.9 convert_reduce_fusion
  315.2 4.8 fusion.2
  323.0 4.3 add_convert_fusion
  327.3 3.0 copy.369
  330.4 5.2 reshape.550
  335.6 8.0 multiply_convert_fusion.2
  343.6 5.9 convert_reduce_fusion.1
  351.3 5.1 fusion.81
  356.4 7.2 reshape.552
  363.6 9.2 copy.375
  372.9 175.0 %all-reduce.7.cloned.1.call-done = f32[12,198,768]{2,0,1:T(8,128)} async-done(((f32[12,198,768]{2,0,1:T(8,128)}), f32[12,198,768]{2,0,1:T(8,128)}) %all-reduce.7.cloned.1.call-update) | async-done | bytes 7299088 | tf_op jit(solution)/shard_map/psum | solution.py:207
  548.0 15.3 %fusion.66 = (f32[768]{0:T(1024)S(1)}, f32[768]{0:T(1024)S(1)}, f32[12,198]{0,1:T(8,128)S(1)}, f32[12,198]{0,1:T(8,128)S(1)}, f32[12,198,768]{2,0,1:T(8,128)}, /*index=5*/f32[12,198,768]{2,0,1:T(8,128)}) fusion(f32[12,198,768]{2,0,1:T(8,128)} %all-reduce.7.cloned.1.call-done, f32[12,198]{0,1:T(8,128)S(1)} %copy-done.32, f32[12,198]{0,1:T(8,128)S(1)} %copy-done.31, ...), kind=kLoop, calls=%fused_computation.175 | loop fusion | flops 18241392 | bytes 25593984 | tf_op jit(solution)/shard_map/reduce_sum | solution.py:209
  563.6 6.7 fusion.68
  573.5 4.2 copy.380
  578.5 36.9 %all-gather.11.cloned.1.call-done = bf16[12,198,768]{1,2,0:T(8,128)(2,1)} async-done(((bf16[12,198,192]{1,2,0:T(8,128)(2,1)}), bf16[12,198,768]{1,2,0:T(8,128)(2,1)}) %all-gather.11.cloned.1.call-update) | async-done | bytes 3649552 | tf_op jit(solution)/shard_map/all_gather | solution.py:213
  615.4 6.6 copy.381
  621.9 5.1 reshape.553
  627.0 3.4 convolution_convert_fusion.1
  630.5 4.5 reshape.554
  635.0 5.3 fusion.5
  640.4 5.2 multiply_reduce_fusion.4
  656.2 5.3 fusion.82
  661.5 5.5 reshape.564
  672.1 7.2 convolution_convert_fusion
  679.3 5.1 convert_element_type.206
  684.4 8.5 copy.370
  692.9 8.0 fusion.88
  700.9 4.8 fusion.87
  707.0 13.3 %psum.178 = f32[12,768]{1,0:T(8,128)S(1)} all-reduce(f32[12,768]{1,0:T(8,128)S(1)} %dynamic_update_slice.3), channel_id=1, replica_groups=mesh['narrow'=8,'wide'=4] {'wide'}, use_global_device_ids=true, to_apply=%region_23.24 | all-reduce | flops 9216 | bytes 73728 | tf_op jit(solution)/shard_map/psum | solution.py:253
  720.4 6.7 copy.400
  727.0 8.5 convert_element_type.228
  735.5 4.3 fusion.86
  739.9 5.8 fusion.85
  745.7 53.9 %all-reduce.9.cloned.1.call-done = f32[12,198,768]{2,1,0:T(8,128)} async-done(((f32[12,198,768]{2,1,0:T(8,128)}), f32[12,198,768]{2,1,0:T(8,128)}) %all-reduce.9.cloned.1.call-update) | async-done | bytes 7299088 | tf_op jit(solution)/shard_map/psum | solution.py:253
  799.6 7.7 multiply_reduce_fusion.2
  807.5 7.8 subtract_multiply_fusion
  815.3 2.9 copy-done.10
  821.1 4.5 collective-permute-start.3
  827.8 12.4 psum.179
  844.2 17.6 %reduce-scatter.5.cloned.1.call-done = bf16[12,198,192]{1,0,2:T(8,128)(2,1)} async-done(((bf16[12,198,768]{1,0,2:T(8,128)(2,1)}), bf16[12,198,192]{1,0,2:T(8,128)(2,1)}) %reduce-scatter.5.cloned.1.call-update) | async-done | bytes 912400 | tf_op jit(solution)/shard_map/reduce_scatter | solution.py:171
  864.0 3.0 fusion.19
  890.0 41.5 %all-reduce.1 = (f32[768]{0:T(1024)}, f32[768]{0:T(1024)}, f32[768]{0:T(1024)}, f32[2,192]{1,0:T(2,128)}, f32[768]{0:T(1024)}, /*index=5*/f32[768]{0:T(1024)}, f...) all-reduce(f32[768]{0:T(1024)S(1)} %get-tuple-element.250, ...), channel_id=1, replica_groups=mesh['narrow'=8,'wide'=4] {'narrow'}, use_global_device_ids=true, to_apply=%region_30.31 | all-reduce | flops 8064 | bytes 64512 | tf_op jit(solution)/shard_map/psum | solution.py:309
  931.5 305.1 %all-reduce.11.cloned.1.call-done = (f32[768,768]{0,1:T(8,128)}, f32[768,3,192]{0,2,1:T(8,128)}, f32[192,768]{1,0:T(8,128)}, f32[768,3,192]{0,2,1:T(8,128)}, f32...) async-done(((f32[768,768]{0,1:T(8,128)}, f32[768,3,192]{0,2,1:T(8,128)}, f32[192,768]{1,0:T(8,128)}, f32[768,3,192]{0,2,1:T(8,128)}, f32[192,768]{1,0:T(8,128)}, ...) | async-done | bytes 11796496 | tf_op jit(solution)/shard_map/psum | solution.py:309
  1236.7 3.2 copy.407
  1239.9 2.9 copy.471
  (346 shorter events, 105.7 us)
Async XLA Ops:
  7.2 328.3 %copy-start = (bf16[768,768]{1,0:T(8,128)(2,1)S(1)}, bf16[768,768]{1,0:T(8,128)(2,1)}, u32[]{:S(2)}) copy-start(bf16[768,768]{1,0:T(8,128)(2,1)} %param.46) | copy-start | bytes 3538948
  7.2 42.6 %all-gather.5.cloned.1.call-start = ((), (), s32[]{:S(2)}) async-start(), calls=%async_computation.2 | async-start | bytes 5898240 | tf_op jit(solution)/shard_map/all_gather | solution.py:95
  7.9 212.8 %reduce-scatter.3.cloned.1.call-start = ((), (), s32[]{:S(2)}) async-start(), calls=%async_computation.3 | async-start | bytes 15728640 | tf_op jit(solution)/shard_map/reduce_scatter | solution.py:157
  9.4 94.7 %copy-start.71 = (f32[3,64]{1,0:T(4,128)}, f32[3,64]{1,0:T(4,128)S(1)}, u32[]{:S(2)}) copy-start(f32[3,64]{1,0:T(4,128)S(1)} %add.320) | copy-start | bytes 2308
  9.5 91.1 %copy-start.60 = (f32[3,64]{1,0:T(4,128)}, f32[3,64]{1,0:T(4,128)S(1)}, u32[]{:S(2)}) copy-start(f32[3,64]{1,0:T(4,128)S(1)} %add.323) | copy-start | bytes 2308
  11.3 43.9 %copy-start.50 = (f32[768]{0:T(1024)S(1)}, f32[768]{0:T(1024)}, u32[]{:S(2)}) copy-start(f32[768]{0:T(1024)} %param.32) | copy-start | bytes 9220
  11.3 43.9 %copy-start.63 = (f32[768]{0:T(1024)S(1)}, f32[768]{0:T(1024)}, u32[]{:S(2)}) copy-start(f32[768]{0:T(1024)} %param.33) | copy-start | bytes 9220
  55.0 33.3 %copy-start.24 = (f32[12,768]{1,0:T(8,128)}, f32[12,768]{1,0:T(8,128)S(1)}, u32[]{:S(2)}) copy-start(f32[12,768]{1,0:T(8,128)S(1)} %get-tuple-element.275) | copy-start | bytes 110596
  57.5 18.7 %collective-permute-start.1 = (bf16[2,12,192]{2,1,0:T(8,128)(2,1)S(1)}, bf16[2,12,192]{2,1,0:T(8,128)(2,1)S(1)}, u32[]{:S(2)}, u32[]{:S(2)}) collective-permute-start(bf16[2,12,192]{2,1,0:T(8,128)(2,1)S(1)} %pad_maximum_fusion.2), channel_id=1, source_target_pairs={{4,0},{8,4},{12,8},{16,12},{20,16},{24,20},{28,24},{5,1},{9,5},{13... | collective-permute-start | bytes 27656 | tf_op jit(solution)/shard_map/ppermute | solution.py:16
  58.8 17.3 %collective-permute-start = (bf16[2,12,192]{2,1,0:T(8,128)(2,1)S(1)}, bf16[2,12,192]{2,1,0:T(8,128)(2,1)S(1)}, u32[]{:S(2)}, u32[]{:S(2)}) collective-permute-start(bf16[2,12,192]{2,1,0:T(8,128)(2,1)S(1)} %pad_maximum_fusion.2), channel_id=1, source_target_pairs={{0,4},{4,8},{8,12},{12,16},{16,20},{20,24},{24,28},{1,5},{5,9},{9,... | collective-permute-start | bytes 27656 | tf_op jit(solution)/shard_map/ppermute | solution.py:16
  64.1 12.2 copy-start.67
  70.5 5.8 copy-start.81
  70.5 7.0 copy-start.33
  70.5 17.8 %copy-start.74 = (f32[768]{0:T(1024)S(1)}, f32[768]{0:T(1024)}, u32[]{:S(2)}) copy-start(f32[768]{0:T(1024)} %param.37) | copy-start | bytes 9220
  76.4 15.8 %copy-start.56 = (bf16[36,3,64]{2,1,0:T(4,128)(2,1)}, bf16[36,3,64]{2,1,0:T(4,128)(2,1)S(1)}, u32[]{:S(2)}) copy-start(bf16[36,3,64]{2,1,0:T(4,128)(2,1)S(1)} %reshape.547) | copy-start | bytes 41476
  77.2 15.0 %copy-start.79 = (f32[3,12]{1,0:T(4,128)}, f32[3,12]{1,0:T(4,128)S(1)}, u32[]{:S(2)}) copy-start(f32[3,12]{1,0:T(4,128)S(1)} %fusion.49) | copy-start | bytes 436
  77.6 14.6 %copy-start.48 = (bf16[12,192]{1,0:T(8,128)(2,1)}, bf16[12,192]{1,0:T(8,128)(2,1)S(1)}, u32[]{:S(2)}) copy-start(bf16[12,192]{1,0:T(8,128)(2,1)S(1)} %convert_element_type.193) | copy-start | bytes 13828
  88.4 6.8 copy-start.28
  120.6 5.9 copy-start.86
  120.6 139.8 %all-gather.9.cloned.1.call-start = ((), (), s32[]{:S(2)}) async-start(), calls=%async_computation.6 | async-start | bytes 5898240 | tf_op jit(solution)/shard_map/all_gather | solution.py:196
  137.4 86.9 %copy-start.83 = (f32[192]{0:T(256)S(1)}, f32[192]{0:T(256)}, u32[]{:S(2)}) copy-start(f32[192]{0:T(256)} %param.43) | copy-start | bytes 2308
  137.4 162.5 %all-gather.7.cloned.1.call-start = ((), (), s32[]{:S(2)}) async-start(), calls=%async_computation.4 | async-start | bytes 5898240 | tf_op jit(solution)/shard_map/all_gather | solution.py:165
  232.6 315.4 %all-reduce.7.cloned.1.call-start = ((), (), s32[]{:S(2)}) async-start(), calls=%async_computation.7 | async-start | bytes 19464192 | tf_op jit(solution)/shard_map/psum | solution.py:207
  335.5 8.0 copy-start.20
  335.5 8.0 copy-start.87
  372.9 175.1 %copy-start.31 = (f32[12,198]{0,1:T(8,128)S(1)}, f32[12,198]{0,1:T(8,128)}, u32[]{:S(2)}) copy-start(f32[12,198]{0,1:T(8,128)} %copy.366) | copy-start | bytes 28516
  372.9 175.1 %copy-start.32 = (f32[12,198]{0,1:T(8,128)S(1)}, f32[12,198]{0,1:T(8,128)}, u32[]{:S(2)}) copy-start(f32[12,198]{0,1:T(8,128)} %copy.368) | copy-start | bytes 28516
  372.9 175.1 %copy-start.62 = (f32[768]{0:T(1024)S(1)}, f32[768]{0:T(1024)}, u32[]{:S(2)}) copy-start(f32[768]{0:T(1024)} %param.44) | copy-start | bytes 9220
  372.9 242.5 %all-gather.11.cloned.1.call-start = ((), (), s32[]{:S(2)}) async-start(), calls=%async_computation.8 | async-start | bytes 5898240 | tf_op jit(solution)/shard_map/all_gather | solution.py:213
  572.1 5.7 copy-start.39
  572.1 5.7 copy-start.47
  577.7 221.8 %all-reduce.9.cloned.1.call-start = ((), (), s32[]{:S(2)}) async-start(), calls=%async_computation.9 | async-start | bytes 14745600 | tf_op jit(solution)/shard_map/psum | solution.py:253
  635.0 10.6 slice-start
  661.5 200.3 %reduce-scatter.5.cloned.1.call-start = ((), (), s32[]{:S(2)}) async-start(), calls=%async_computation.5 | async-start | bytes 7864320 | tf_op jit(solution)/shard_map/reduce_scatter | solution.py:171
  692.9 8.0 copy-start.21
  692.9 8.0 copy-start.92
  705.8 530.9 %all-reduce.11.cloned.1.call-start = ((), (), s32[]{:S(2)}) async-start(), calls=%async_computation.10 | async-start | bytes 23592960 | tf_op jit(solution)/shard_map/psum | solution.py:309
  727.0 8.5 copy-start.19
  739.8 59.8 %copy-start.29 = (f32[12,1,768]{2,1,0:T(1,128)S(1)}, f32[12,1,768]{2,1,0:T(1,128)}, u32[]{:S(2)}) copy-start(f32[12,1,768]{2,1,0:T(1,128)} %copy-done.28) | copy-start | bytes 110596
  739.8 59.8 %copy-start.41 = (f32[12,198]{1,0:T(8,128)S(1)}, f32[12,198]{1,0:T(8,128)}, u32[]{:S(2)}) copy-start(f32[12,198]{1,0:T(8,128)} %copy-done.40) | copy-start | bytes 28516
  739.8 59.8 %copy-start.44 = (f32[12,198]{1,0:T(8,128)S(1)}, f32[12,198]{1,0:T(8,128)}, u32[]{:S(2)}) copy-start(f32[12,198]{1,0:T(8,128)} %copy-done.43) | copy-start | bytes 28516
  739.8 59.8 %copy-start.53 = (f32[768]{0:T(1024)S(1)}, f32[768]{0:T(1024)}, u32[]{:S(2)}) copy-start(f32[768]{0:T(1024)} %param.38) | copy-start | bytes 9220
  799.6 7.8 copy-start.5
  807.4 10.9 copy-start.34
  807.4 11.2 copy-start.57
  807.4 11.2 copy-start.59
  807.4 11.2 copy-start.78
  807.4 11.2 copy-start.80
  807.5 11.4 copy-start.68
  807.5 18.2 %copy-start.49 = (bf16[12,192]{1,0:T(8,128)(2,1)S(1)}, bf16[12,192]{1,0:T(8,128)(2,1)}, u32[]{:S(2)}) copy-start(bf16[12,192]{1,0:T(8,128)(2,1)} %copy-done.48) | copy-start | bytes 13828
  807.5 19.3 %copy-start.55 = (bf16[36,3,64]{2,1,0:T(4,128)(2,1)S(1)}, bf16[36,3,64]{2,1,0:T(4,128)(2,1)}, u32[]{:S(2)}) copy-start(bf16[36,3,64]{2,1,0:T(4,128)(2,1)} %copy-done.54) | copy-start | bytes 41476
  807.5 20.0 %copy-start.23 = (bf16[768,3,192]{0,2,1:T(8,128)(2,1)S(1)}, bf16[768,3,192]{0,2,1:T(8,128)(2,1)}, u32[]{:S(2)}) copy-start(bf16[768,3,192]{0,2,1:T(8,128)(2,1)} %param.34) | copy-start | bytes 2654212
  818.2 22.0 %copy-start.25 = (f32[12,768]{1,0:T(8,128)S(1)}, f32[12,768]{1,0:T(8,128)}, u32[]{:S(2)}) copy-start(f32[12,768]{1,0:T(8,128)} %copy-done.24) | copy-start | bytes 110596
  818.2 22.0 %copy-start.51 = (f32[768]{0:T(1024)S(1)}, f32[768]{0:T(1024)}, u32[]{:S(2)}) copy-start(f32[768]{0:T(1024)} %param.32) | copy-start | bytes 9220
  818.2 22.0 %copy-start.66 = (f32[12]{0:T(128)S(1)}, f32[12]{0:T(128)}, u32[]{:S(2)}) copy-start(f32[12]{0:T(128)} %copy-done.65) | copy-start | bytes 148
  818.2 22.0 %copy-start.70 = (f32[12]{0:T(128)S(1)}, f32[12]{0:T(128)}, u32[]{:S(2)}) copy-start(f32[12]{0:T(128)} %copy-done.69) | copy-start | bytes 148
  818.2 22.3 %copy-start.64 = (f32[768]{0:T(1024)S(1)}, f32[768]{0:T(1024)}, u32[]{:S(2)}) copy-start(f32[768]{0:T(1024)} %param.33) | copy-start | bytes 9220
  818.2 24.0 %copy-start.45 = (bf16[12,1,768]{2,0,1:T(8,128)(2,1)S(1)}, bf16[12,1,768]{2,0,1:T(8,128)(2,1)}, u32[]{:S(2)}) copy-start(bf16[12,1,768]{2,0,1:T(8,128)(2,1)} %copy.415) | copy-start | bytes 55300
  819.8 7.3 collective-permute-start.2
  821.1 6.1 collective-permute-start.3
  844.1 19.9 %copy-start.82 = (f32[192]{0:T(256)S(1)}, f32[192]{0:T(256)}, u32[]{:S(2)}) copy-start(f32[192]{0:T(256)} %param.49) | copy-start | bytes 2308
  870.2 7.4 copy-start.18
  1236.7 6.1 copy-start.37
  1236.7 6.9 copy-start.30
  (45 other events, 130.8 us)
Sparse Core Ops, SparseCore 0:
  9.6 40.1 all-gather.4
  120.7 99.9 reduce-scatter.2
  222.9 37.4 all-gather.8
  262.4 37.4 all-gather.6
  373.0 174.9 all-reduce.6
  577.9 37.4 all-gather.10
  661.6 137.9 all-reduce.8
  802.3 59.4 reduce-scatter.4
  868.8 367.7 all-reduce.10
where the time goes:
time: 1260 us
  waiting for transfers between devices  767 us (61%)
  local copies, waits for them, and re-layouts  202 us (16%)
  matrix products  90.6 us (7%)
  other arithmetic  89.8 us (7%)
  blocking collectives  77.8 us (6%)
  between operations  16.2 us (1%)
    psum x1, waiting for transfers between devices, body(): lax.psum((grad_message_weight, grad_message_bias, grad_message_gain, grad...  305 us
    psum x1, waiting for transfers between devices, body(): grad_mlp_in = lax.psum(norm_term, 'wide')  175 us
    reduce_scatter x1, waiting for transfers between devices, body(): lax.psum_scatter(mat_mul(attn_mix, out_weight).reshape(frames, seq_len, m...  83.3 us
    psum x1, waiting for transfers between devices, body(): lax.psum((mat_nt(grad_proj, qkv_flat).reshape(frames, seq_len, model_widt...  53.9 us
    psum x1, blocking collectives, body(): lax.psum((grad_message_weight, grad_message_bias, grad_message_gain, grad...  41.5 us
    all_gather x1, waiting for transfers between devices, body(): full_tokens = lax.all_gather(frame_tokens, 'wide', axis=2, tiled=True)  38.5 us
    unnamed x202, local copies, waits for them, and re-layouts  38.1 us
    all_gather x1, waiting for transfers between devices, body(): lax.all_gather(grad_hidden.astype(low_type), 'wide', axis=2, tiled=True)  36.9 us
  transfers between devices with their start and end apart: 13, of which 10 were waited for; matrix products, arithmetic and copies ran while one was open for 14% of the time, Pallas kernels for 0%

commit v1 on v0

v1 whole, which is shorter than its diff:
```python
import jax
import jax.numpy as jnp
from jax import lax
from jax.sharding import PartitionSpec as P


VIDEO_FRAMES = 8
HD = 64
EPS = 1e-05
ROW_TILE = 16
LOW = jnp.bfloat16
F32 = jnp.float32


def dot(left, right, dims):
    return lax.dot_general(left, right, (dims, ((), ())), preferred_element_type=F32)


def mat_mul(left, right):
    return dot(left, right, ((1,), (0,)))


def mat_tn(left, right):
    return dot(left, right, ((0,), (0,)))


def mat_nt(left, right):
    return dot(left, right, ((1,), (1,)))


def normalize(values):
    row_mean = jnp.mean(values, axis=-1, keepdims=True)
    centred = values - row_mean
    inv_std = lax.rsqrt(jnp.mean(centred * centred, axis=-1, keepdims=True) + EPS)
    return (centred * inv_std, inv_std)


def norm_back(grad_norm, normed, inv_std, norm_gain):
    scaled = grad_norm * norm_gain
    return inv_std * (
        scaled
        - jnp.mean(scaled, axis=-1, keepdims=True)
        - normed * jnp.mean(scaled * normed, axis=-1, keepdims=True)
    )


def swap(block, axis, flip):
    return lax.ppermute(block, axis, [(i, i ^ flip) for i in range(lax.axis_size(axis))])


def bits_of(size):
    return [1 << b for b in range(size.bit_length() - 1)]


def reorder(parts, index):
    parts = list(parts)
    for bit in bits_of(len(parts)):
        odd = (index & bit) != 0
        parts = [jnp.where(odd, parts[k ^ bit], parts[k]) for k in range(len(parts))]
    return parts


def gather_all(block, axis, order):
    index = lax.axis_index(axis)
    for bit in order:
        other = swap(block, axis, bit)
        odd = (index & bit) != 0
        block = jnp.concatenate(
            [jnp.where(odd, other, block), jnp.where(odd, block, other)], axis=0
        )
    return block


def sum_all(block, axis):
    for bit in bits_of(lax.axis_size(axis)):
        block = block + swap(block, axis, bit)
    return block


def frames_in(block, count, index):
    part = block.shape[0] // count
    pieces = []
    for k in range(count):
        piece = lax.dynamic_slice_in_dim(block, (index ^ k) * part, part, 0)
        pieces.append(piece if k == 0 else swap(piece, "wide", k))
    return jnp.concatenate(reorder(pieces, index), axis=2)


def frames_out(block, count, index):
    width = block.shape[2] // count
    pieces = reorder([block[:, :, j * width : (j + 1) * width] for j in range(count)], index)
    pieces = [piece if k == 0 else swap(piece, "wide", k) for k, piece in enumerate(pieces)]
    return jnp.concatenate(reorder(pieces, index), axis=0)


def shards_in(block, count):
    shards = {0: block}
    for bit in reversed(bits_of(count)):
        for k in list(shards):
            shards[k ^ bit] = swap(shards[k], "wide", bit)
    return [shards[k] for k in range(count)]


def reduce_grad(parts):
    parts = {k: part for k, part in enumerate(parts)}
    for bit in bits_of(len(parts)):
        away = [k for k in parts if k & bit]
        sent = swap(jnp.concatenate([parts[k] for k in away], axis=0), "wide", bit)
        size = parts[0].shape[0]
        parts = {
            k ^ bit: (
                parts[k ^ bit].astype(F32) + sent[at * size : (at + 1) * size].astype(F32)
            ).astype(LOW)
            for at, k in enumerate(away)
        }
    block = parts[0]
    index = lax.axis_index("narrow")
    bits = bits_of(lax.axis_size("narrow"))
    for bit in bits:
        odd = (index & bit) != 0
        half = block.shape[0] // 2
        low, high = block[:half], block[half:]
        other = swap(jnp.where(odd, low, high), "narrow", bit)
        block = (jnp.where(odd, high, low).astype(F32) + other.astype(F32)).astype(LOW)
    for bit in reversed(bits):
        odd = (index & bit) != 0
        other = swap(block, "narrow", bit)
        block = jnp.concatenate(
            [jnp.where(odd, other, block), jnp.where(odd, block, other)], axis=0
        )
    return block.astype(F32)


def body(
    frame_tokens,
    cotangent,
    caption_count,
    caption_len,
    message_weight,
    message_bias,
    message_gain,
    message_shift,
    cross_qkv,
    cross_bias,
    cross_proj,
    cross_offset,
    attn_gain,
    attn_shift,
    qkv_weight,
    qkv_bias,
    out_weight,
    out_bias,
    mlp_gain,
    mlp_shift,
    up_weight,
    up_bias,
    down_weight,
    down_bias,
):
    group_frames, patches, width_part = frame_tokens.shape
    model_width = message_weight.shape[0]
    hidden_part = up_weight.shape[1]
    wide = lax.axis_size("wide")
    narrow = lax.axis_size("narrow")
    wide_idx = lax.axis_index("wide")
    narrow_idx = lax.axis_index("narrow")
    frames = group_frames // wide
    seq_len = patches + 1
    seq_pad = -(-seq_len // ROW_TILE) * ROW_TILE
    rows = frames * seq_pad
    part_heads = width_part // HD
    score_scale = HD ** (-0.5)
    all_frames = group_frames * narrow
    first_group = narrow_idx * group_frames
    first_frame = first_group + wide_idx * frames

    tokens = frames_in(frame_tokens, wide, wide_idx)
    cls_part = frame_tokens[:, 0, :]
    cls_rows = jnp.concatenate(
        reorder([cls_part] + [swap(cls_part, "wide", k) for k in range(1, wide)], wide_idx), axis=1
    )
    cls_rows = gather_all(cls_rows, "narrow", bits_of(narrow))
    qkv_shards = shards_in(qkv_weight.reshape(model_width, 3 * width_part), wide)
    rest_shards = shards_in(jnp.concatenate([out_weight, up_weight, down_weight], axis=0), wide)
    cot = frames_in(cotangent, wide, wide_idx)

    message = mat_mul(cls_rows, message_weight) + message_bias
    msg_normed, msg_inv = normalize(message)
    msg_in = (msg_normed * message_gain + message_shift).astype(LOW)
    cross_flat = cross_qkv.reshape(model_width, 3 * width_part)
    cross_all = mat_mul(msg_in, cross_flat)
    cross_query = (cross_all[:, :width_part] + cross_bias[0]).astype(LOW)
    cross_key = cross_all[:, width_part : 2 * width_part].astype(LOW)
    cross_value = (cross_all[:, 2 * width_part :] + cross_bias[1]).astype(LOW)
    chunk = max(c for c in range(VIDEO_FRAMES, 129, VIDEO_FRAMES) if all_frames % c == 0)
    chunks = all_frames // chunk

    def by_head(values):
        return values.reshape(chunks, chunk, part_heads, HD)

    def from_head(values):
        return values.reshape(all_frames, width_part)

    def ein(expr, left, right):
        return jnp.einsum(expr, left, right, preferred_element_type=F32)

    video_of = jnp.arange(chunk) // VIDEO_FRAMES
    same_video = video_of[:, None] == video_of[None, :]
    query_heads, key_heads, value_heads = by_head(cross_query), by_head(cross_key), by_head(cross_value)
    cross_score = ein("cthd,cuhd->chtu", query_heads, key_heads) * score_scale
    cross_prob = jax.nn.softmax(jnp.where(same_video, cross_score, -1e30), axis=-1)
    cross_mix = from_head(ein("chtu,cuhd->cthd", cross_prob.astype(LOW), value_heads)).astype(LOW)
    group_mix = lax.dynamic_slice_in_dim(cross_mix, first_group, group_frames, 0)
    group_sum = mat_mul(group_mix, cross_proj)
    message_two = lax.dynamic_slice_in_dim(message, first_frame, frames, 0) + cross_offset
    for k in range(wide):
        piece = lax.dynamic_slice_in_dim(group_sum, (wide_idx ^ k) * frames, frames, 0)
        message_two = message_two + (piece if k == 0 else swap(piece, "wide", k))

    full_cat = jnp.concatenate(
        [
            tokens.astype(F32),
            message_two[:, None, :],
            jnp.zeros((frames, seq_pad - seq_len, model_width), F32),
        ],
        axis=1,
    ).reshape(rows, model_width)
    attn_normed, attn_inv = normalize(full_cat)
    attn_in = (attn_normed * attn_gain + attn_shift).astype(LOW)
    qkv_full = jnp.concatenate(qkv_shards, axis=1)
    qkv_bias_all = jnp.stack(shards_in(qkv_bias, wide))
    up_bias_all = jnp.concatenate(shards_in(up_bias, wide))
    out_bias_all = jnp.concatenate(reorder(shards_in(out_bias, wide), wide_idx))
    down_bias_all = jnp.concatenate(reorder(shards_in(down_bias, wide), wide_idx))
    heads = wide * part_heads
    proj = mat_mul(attn_in, qkv_full).reshape(rows, wide, 3, width_part)

    def heads_of(values):
        return values.astype(LOW).reshape(frames, seq_pad, heads, HD)

    queries = heads_of(proj[:, :, 0] + qkv_bias_all[:, 0])
    keys = heads_of(proj[:, :, 1])
    values = heads_of(proj[:, :, 2] + qkv_bias_all[:, 1])
    scores = ein("tshd,tuhd->thsu", queries, keys) * score_scale
    scores = jnp.where(jnp.arange(seq_pad) < seq_len, scores, -1e30)
    prob = jax.nn.softmax(scores, axis=-1)
    prob_low = prob.astype(LOW)
    attn_mix = ein("thsu,tuhd->tshd", prob_low, values).astype(LOW).reshape(rows, model_width)
    out_full = jnp.concatenate([s[:width_part] for s in rest_shards], axis=0)
    up_full = jnp.concatenate([s[width_part : width_part + model_width] for s in rest_shards], axis=1)
    down_full = jnp.concatenate([s[width_part + model_width :] for s in rest_shards], axis=0)
    hidden_res = full_cat + mat_mul(attn_mix, out_full) + out_bias_all
    mlp_normed, mlp_inv = normalize(hidden_res.astype(LOW).astype(F32))
    mlp_in = (mlp_normed * mlp_gain + mlp_shift).astype(LOW)
    pre_act = mat_mul(mlp_in, up_full) + up_bias_all
    gate_sig = jax.nn.sigmoid(1.702 * pre_act)
    activated = (pre_act * gate_sig).astype(LOW)
    result = hidden_res + mat_mul(activated, down_full) + down_bias_all
    result = result.reshape(frames, seq_pad, model_width)[:, :patches].astype(LOW)
    output_tokens = frames_out(result, wide, wide_idx)

    caption_slot = jnp.arange(caption_len.shape[1])
    word_total = jnp.sum(
        jnp.where(caption_slot[None, :] < caption_count[:, None], caption_len, 0), axis=1
    ).astype(F32)
    video_scale = word_total / jnp.mean(word_total)
    own_video = (first_frame + jnp.arange(frames)) // VIDEO_FRAMES
    video_match = own_video[:, None] == jnp.arange(video_scale.shape[0])[None, :]
    frame_weight = jnp.sum(jnp.where(video_match, video_scale[None, :], 0.0), axis=1)
    grad_res = jnp.concatenate(
        [
            cot.astype(F32) * frame_weight[:, None, None],
            jnp.zeros((frames, seq_pad - patches, model_width), F32),
        ],
        axis=1,
    ).reshape(rows, model_width)
    grad_rows = grad_res.astype(LOW)
    sum_down_bias = jnp.sum(grad_res, axis=0)
    grad_down = mat_tn(activated, grad_rows).astype(LOW)
    grad_act = mat_nt(grad_rows, down_full)
    grad_pre = (grad_act * (gate_sig + 1.702 * pre_act * gate_sig * (1.0 - gate_sig))).astype(LOW)
    sum_up_bias = jnp.sum(grad_pre, axis=0, dtype=F32)
    grad_up = mat_tn(mlp_in, grad_pre).astype(LOW)
    grad_down_own = reduce_grad([grad_down[k * hidden_part : (k + 1) * hidden_part] for k in range(wide)])
    grad_up_own = reduce_grad([grad_up[:, k * hidden_part : (k + 1) * hidden_part] for k in range(wide)])
    grad_mlp_in = mat_nt(grad_pre, up_full)
    sum_mlp_gain = jnp.sum(grad_mlp_in * mlp_normed, axis=0)
    sum_mlp_shift = jnp.sum(grad_mlp_in, axis=0)
    grad_hidden = grad_res + norm_back(grad_mlp_in, mlp_normed, mlp_inv, mlp_gain)
    sum_out_bias = jnp.sum(grad_hidden, axis=0)
    grad_low = grad_hidden.astype(LOW)
    grad_out = mat_tn(attn_mix, grad_low).astype(LOW)
    grad_out_own = reduce_grad([grad_out[k * width_part : (k + 1) * width_part] for k in range(wide)])
    grad_mix = mat_nt(grad_low, out_full).astype(LOW).reshape(frames, seq_pad, heads, HD)
    grad_value = ein("thsu,tshd->tuhd", prob_low, grad_mix)
    grad_prob = ein("tshd,tuhd->thsu", grad_mix, values)
    grad_score = (prob * (grad_prob - jnp.sum(prob * grad_prob, axis=-1, keepdims=True))).astype(LOW)
    grad_query = ein("thsu,tuhd->tshd", grad_score, keys) * score_scale
    grad_key = ein("thsu,tshd->tuhd", grad_score, queries) * score_scale
    grad_proj = (
        jnp.stack(
            [g.reshape(rows, wide, width_part) for g in (grad_query, grad_key, grad_value)], axis=2
        )
        .astype(LOW)
        .reshape(rows, wide * 3 * width_part)
    )
    sum_proj = jnp.sum(grad_proj, axis=0, dtype=F32).reshape(wide, 3, width_part)
    grad_qkv = mat_tn(attn_in, grad_proj).astype(LOW)
    grad_qkv_own = reduce_grad(
        [grad_qkv[:, k * 3 * width_part : (k + 1) * 3 * width_part] for k in range(wide)]
    )
    grad_attn_in = mat_nt(grad_proj, qkv_full)
    sum_attn_gain = jnp.sum(grad_attn_in * attn_normed, axis=0)
    sum_attn_shift = jnp.sum(grad_attn_in, axis=0)
    grad_total = (
        norm_back(grad_attn_in, attn_normed, attn_inv, attn_gain) + grad_hidden
    ).reshape(frames, seq_pad, model_width)
    grad_tokens = frames_out(grad_total[:, :patches].astype(LOW), wide, wide_idx)

    sums = jnp.concatenate(
        [sum_down_bias, sum_mlp_gain, sum_mlp_shift, sum_out_bias, sum_attn_gain, sum_attn_shift]
        + reorder([sum_up_bias[k * hidden_part : (k + 1) * hidden_part] for k in range(wide)], wide_idx)
        + reorder([sum_proj[k, 0] for k in range(wide)], wide_idx)
        + reorder([sum_proj[k, 2] for k in range(wide)], wide_idx)
    )
    sums = sum_all(sum_all(sums.reshape(-1, 128), "wide"), "narrow").reshape(-1)
    sums = [sums[at : at + model_width] for at in range(0, sums.shape[0], model_width)]
    grad_down_bias, grad_mlp_gain, grad_mlp_shift, grad_out_bias, grad_attn_gain, grad_attn_shift = sums[:6]
    hidden_sums = jnp.concatenate(sums[6:-2])
    grad_up_bias = lax.dynamic_slice_in_dim(hidden_sums, wide_idx * hidden_part, hidden_part, 0)
    col_start = wide_idx * width_part

    def own_cols(values):
        return lax.dynamic_slice_in_dim(values, col_start, width_part, values.ndim - 1)

    grad_qkv_bias = own_cols(jnp.stack(sums[-2:]))

    grad_message_two = gather_all(
        gather_all(grad_total[:, patches], "wide", bits_of(wide)), "narrow", bits_of(narrow)
    )
    grad_cross = grad_message_two.astype(LOW)
    grad_cross_offset = jnp.sum(grad_cross, axis=0, dtype=F32)
    grad_cross_proj = mat_tn(cross_mix, grad_cross)
    grad_cross_mix = by_head(mat_nt(grad_cross, cross_proj).astype(LOW))
    grad_cross_prob = ein("cthd,cuhd->chtu", grad_cross_mix, value_heads)
    grad_cross_score = cross_prob * (
        grad_cross_prob - jnp.sum(cross_prob * grad_cross_prob, axis=-1, keepdims=True)
    )
    score_low = grad_cross_score.astype(LOW)
    grad_cross_all = jnp.concatenate(
        [
            from_head(ein("chtu,cuhd->cthd", score_low, key_heads)) * score_scale,
            from_head(ein("chtu,cthd->cuhd", score_low, query_heads)) * score_scale,
            from_head(ein("chtu,cthd->cuhd", cross_prob.astype(LOW), grad_cross_mix)),
        ],
        axis=1,
    ).astype(LOW)
    cross_sums = jnp.sum(grad_cross_all, axis=0, dtype=F32).reshape(3, width_part)
    grad_cross_bias = jnp.stack([cross_sums[0], cross_sums[2]])
    grad_cross_qkv = mat_tn(msg_in, grad_cross_all).reshape(model_width, 3, width_part)
    grad_msg_in = sum_all(mat_nt(grad_cross_all, cross_flat), "wide")
    grad_message_gain = jnp.sum(grad_msg_in * msg_normed, axis=0)
    grad_message_shift = jnp.sum(grad_msg_in, axis=0)
    grad_message = (
        grad_message_two + norm_back(grad_msg_in, msg_normed, msg_inv, message_gain)
    ).astype(LOW)
    grad_message_bias = jnp.sum(grad_message, axis=0, dtype=F32)
    grad_message_weight = mat_tn(cls_rows, grad_message)
    group_message = lax.dynamic_slice_in_dim(grad_message, first_group, group_frames, 0)
    grad_cls = own_cols(mat_nt(group_message, message_weight))
    grad_tokens = grad_tokens.astype(F32).at[:, 0].add(grad_cls).astype(LOW)

    return (
        output_tokens,
        grad_tokens,
        grad_message_weight,
        grad_message_bias,
        grad_message_gain,
        grad_message_shift,
        grad_cross_qkv,
        grad_cross_bias,
        grad_cross_proj,
        grad_cross_offset,
        grad_attn_gain,
        grad_attn_shift,
        grad_qkv_own.reshape(model_width, 3, width_part),
        grad_qkv_bias,
        grad_out_own,
        own_cols(grad_out_bias),
        grad_mlp_gain,
        grad_mlp_shift,
        grad_up_own,
        grad_up_bias,
        grad_down_own,
        own_cols(grad_down_bias),
    )


def solution(mesh):
    return jax.shard_map(
        body,
        mesh=mesh,
        in_specs=(
            P("narrow", None, "wide"),
            P("narrow", None, "wide"),
            P(),
            P(),
            P(),
            P(),
            P(),
            P(),
            P(None, None, "wide"),
            P(None, "wide"),
            P("wide", None),
            P(),
            P(),
            P(),
            P(None, None, "wide"),
            P(None, "wide"),
            P("wide", None),
            P("wide"),
            P(),
            P(),
            P(None, "wide"),
            P("wide"),
            P("wide", None),
            P("wide"),
        ),
        out_specs=(
            P("narrow", None, "wide"),
            P("narrow", None, "wide"),
            P(),
            P(),
            P(),
            P(),
            P(None, None, "wide"),
            P(None, "wide"),
            P("wide", None),
            P(),
            P(),
            P(),
            P(None, None, "wide"),
            P(None, "wide"),
            P("wide", None),
            P("wide"),
            P(),
            P(),
            P(None, "wide"),
            P("wide"),
            P("wide", None),
            P("wide"),
        ),
        check_vma=False,
    )
```

time: 1260 us -> 535 us (0.42)
  waiting for transfers between devices: 767 us -> 178 us
  local copies, waits for them, and re-layouts: 202 us -> 101 us
  blocking collectives: 77.8 us -> 0 us
  starting transfers between devices: 12 us -> 68.9 us
    psum x3 -> x0, waiting for transfers between devices: 534 us -> none  [the longest x1 305 us: body(): lax.psum((grad_message_weight, grad_message_bias, grad_message_gain, grad...]
    ppermute x4 -> x83, waiting for transfers between devices: 0.15 us -> 178 us  [swap(): lax.ppermute(block, axis, [(i, i ^ flip) for i in range(lax.axis_size(axi...]
    all_gather x4 -> x0, waiting for transfers between devices: 131 us -> none  [the longest x1 38.5 us: body(): full_tokens = lax.all_gather(frame_tokens, 'wide', axis=2, tiled=True)]
    reduce_scatter x2 -> x0, waiting for transfers between devices: 101 us -> none  [the longest x1 83.3 us: body(): lax.psum_scatter(mat_mul(attn_mix, out_weight).reshape(frames, seq_len, m...]
    psum x4 -> x0, blocking collectives: 77.8 us -> none  [the longest x1 41.5 us: body(): lax.psum((grad_message_weight, grad_message_bias, grad_message_gain, grad...]
    ppermute x4 -> x83, starting transfers between devices: 11.7 us -> 68.9 us  [swap(): lax.ppermute(block, axis, [(i, i ^ flip) for i in range(lax.axis_size(axi...]
    convert_element_type x18 -> x7, local copies, waits for them, and re-layouts: 57.5 us -> 8.59 us  [the longest x1 4.59 us: heads_of(): return values.astype(LOW).reshape(frames, seq_pad, heads, HD)]
    reduce_sum x12 -> x8, other arithmetic: 40.1 us -> 5.83 us  [the longest x1 2.3 us: body(): jnp.sum(grad_proj, axis=0, dtype=F32).reshape(wide, 3, width_part)]
  transfers between devices with their start and end apart: 13 -> 83, of which waited for: 10 -> 37; matrix products, arithmetic and copies ran while one was open for 14% -> 30% of each run, Pallas kernels for 0% -> 0%
where the time goes in v1:
time: 535 us; the launch traced here: 526 us
  waiting for transfers between devices  178 us (33%)
  local copies, waits for them, and re-layouts  101 us (19%)
  matrix products  87 us (16%)
  other arithmetic  86.7 us (16%)
  starting transfers between devices  68.9 us (13%)
    ppermute x83, waiting for transfers between devices, swap(): lax.ppermute(block, axis, [(i, i ^ flip) for i in range(lax.axis_size(axi...  178 us
    ppermute x83, starting transfers between devices, swap(): lax.ppermute(block, axis, [(i, i ^ flip) for i in range(lax.axis_size(axi...  68.9 us
    dot_general x21, matrix products, dot(): lax.dot_general(left, right, (dims, ((), ())), preferred_element_type=F32)  64.1 us
    unnamed x252, local copies, waits for them, and re-layouts  26.8 us
    dot_general x11, matrix products, ein(): return jnp.einsum(expr, left, right, preferred_element_type=F32)  22 us
    convert_element_type x8, other arithmetic, reduce_grad(): parts = {k ^ bit: (parts[k ^ bit].astype(F32) + sent[at * size:(at + 1) *...  12.7 us
  transfers between devices with their start and end apart: 83, of which 37 were waited for; matrix products, arithmetic and copies ran while one was open for 30% of the time, Pallas kernels for 0%

profile of v1, /device:TPU:0, one launch (start us, length us, event | category | flops | bytes accessed | tf_op | source)
XLA Modules:
  0.0 526.1 jit_solution(9966179892978016974)
XLA Ops:
  2.3 2.4 collective-permute-start.3
  33.8 2.2 collective-permute-done.6
  42.1 2.6 collective-permute-start.8
  44.7 4.3 collective-permute-done.8
  63.9 22.3 %collective-permute-done = bf16[3,197,192]{2,1,0:T(8,128)(2,1)S(1)} collective-permute-done((bf16[3,197,192]{2,1,0:T(8,128)(2,1)}, bf16[3,197,192]{2,1,0:T(8,128)(2,1)S(1)}, u32[]{:S(2)}, u32[]{:S(2)}) %collective-permute-start) | collective-permute-done | bytes 226976 | tf_op jit(solution)/shard_map/ppermute | solution.py:48
  86.9 6.7 %collective-permute-done.1 = bf16[3,197,192]{2,1,0:T(8,128)(2,1)S(1)} collective-permute-done((bf16[3,197,192]{2,1,0:T(8,128)(2,1)}, bf16[3,197,192]{2,1,0:T(8,128)(2,1)S(1)}, u32[]{:S(2)}, u32[]{:S(2)}) %collective-permute-start.1) | collective-permute-done | bytes 226976 | tf_op jit(solution)/shard_map/ppermute | solution.py:48
  98.7 3.2 fusion.21
  101.9 2.4 pad_maximum_fusion.2
  104.3 3.0 fusion.108
  107.3 2.4 fusion.94
  110.9 5.0 squeeze.10
  115.9 3.3 add_convert_fusion
  119.1 2.6 slice.851
  121.7 4.9 squeeze.9
  126.7 4.6 convert_element_type.412
  131.2 3.2 fusion.44
  134.5 14.2 %collective-permute-done.19 = bf16[1728,768]{1,0:T(8,128)(2,1)} collective-permute-done((bf16[1728,768]{1,0:T(8,128)(2,1)}, bf16[1728,768]{1,0:T(8,128)(2,1)}, u32[]{:S(2)}, u32[]{:S(2)}) %collective-permute-start.19) | collective-permute-done | bytes 2654240 | tf_op jit(solution)/shard_map/ppermute | solution.py:48
  149.9 3.2 fusion.107
  153.9 2.4 copy-done.10
  158.4 4.0 reshape.592
  166.3 2.2 fusion.98
  174.0 9.0 %multiply_convert_fusion.2 = (bf16[624,3072]{1,0:T(8,128)(2,1)}, f32[624,3072]{1,0:T(8,128)}) fusion(f32[3072]{0:T(1024)S(1)} %pad_maximum_fusion.39, bf16[768,768]{1,0:T(8,128)(2,1)S(1)} %get-tuple-element.164, bf16[768,768]{1,0:T(8,128)(2,1)S(1)} %get-tuple-element.162, bf16[768,768]{1,0:T(8,128)(2,1)S(1)} %get-tuple-element.160, ...), kind=kOutput, calls=%fused_computation.6 | convolution fusion | flops 2979569664 | bytes 17202048 | tf_op jit(solution)/shard_map/dot_general | solution.py:16
  183.1 13.9 %convert_reduce_fusion = (f32[3072]{0:T(1024)S(1)}, bf16[624,3072]{1,0:T(8,128)(2,1)S(1)}) fusion(f32[624,3072]{1,0:T(8,128)} %get-tuple-element.306, f32[3072]{0:T(1024)S(1)} %pad_maximum_fusion.39, bf16[624,768]{1,0:T(8,128)(2,1)S(1)} %copy-done.54, bf16[768,768]{1,0:T(8,128)(2,1)S(1)} %get-tuple-element.163, bf16[768,768]{1,0:T(8,128)(2,1)S(1)} %get-tuple-element.161, ...), kind=kOutput, calls=%fused_computation.2 | convolution fusion | flops 2988192768 | bytes 17203200 | tf_op jit(solution)/shard_map/dot_general | solution.py:16
  197.0 3.6 fusion.18
  203.6 2.9 reshape.603
  206.5 3.4 copy.188
  209.8 5.7 %fusion.26 = bf16[3,208,12,64]{1,3,2,0:T(8,128)(2,1)} fusion(bf16[3,208,12,64]{1,3,2,0:T(8,128)(2,1)S(1)} %copy.188, f32[3,12,208,208]{2,3,1,0:T(8,128)} %copy-done.10, f32[3,12,208]{2,1,0:T(8,128)S(1)} %get-tuple-element.297), kind=kOutput, calls=%fused_computation.73 | convolution fusion | flops 202475520 | bytes 8176896 | tf_op jit(solution)/shard_map/thsu,tshd->tuhd/dot_general | solution.py:205
  215.5 6.3 %multiply_reduce_fusion = (f32[3,12,208]{2,1,0:T(8,128)S(1)}, f32[3,12,208,208]{2,3,1,0:T(8,128)}) fusion(f32[3,12,208,208]{2,3,1,0:T(8,128)} %copy-done.10, f32[3,12,208]{2,1,0:T(8,128)S(1)} %get-tuple-element.297, bf16[3,208,12,64]{1,3,2,0:T(8,128)(2,1)S(1)} %copy.188, bf16[3,208,12,64]{1,0,3,2:T(4,128)(2,1)S(1)} %copy-done.26), kind=kOutput, calls=%fused_computation.4 | convolution fusion | flops 204025536 | bytes 14436864 | tf_op jit(solution)/shard_map/tshd,tuhd->thsu/dot_general | solution.py:205
  221.9 7.5 %multiply_convert_fusion = bf16[3,12,208,208]{2,3,1,0:T(8,128)(2,1)S(1)} fusion(f32[3,12,208,208]{2,3,1,0:T(8,128)} %get-tuple-element.301, f32[3,12,208]{2,1,0:T(8,128)S(1)} %get-tuple-element.300, f32[3,12,208,208]{2,3,1,0:T(8,128)} %copy-done.10, f32[3,12,208]{2,1,0:T(8,128)S(1)} %get-tuple-element.297), kind=kLoop, calls=%fused_computation.3 | loop fusion | flops 6230016 | bytes 15634944 | tf_op jit(solution)/shard_map/convert_element_type | solution.py:297
  229.4 2.3 multiply_bitcast_fusion
  236.6 2.3 copy.195
  240.9 2.3 copy.192
  245.3 2.3 convert_reduce_fusion.1
  247.9 2.8 copy-done.17
  251.2 2.9 multiply_reduce_fusion.1
  258.2 6.2 %convolution_convert_fusion.1 = bf16[768,3072]{1,0:T(8,128)(2,1)} fusion(bf16[624,3072]{1,0:T(8,128)(2,1)S(1)} %copy-done.112, bf16[624,768]{1,0:T(8,128)(2,1)S(1)} %copy-done.9, f32[768]{0:T(1024)S(1)} %copy-done.107, f32[768]{0:T(1024)S(1)} %copy-done.91, f32[624]{0:T(1024)S(1)} %add_rsqrt_fusion, f32[624]{0:T(1024)S(1)} %broadcast_multiply_fusion.4), kind=kOutput, calls=%fused_computation.14 | convolution fusion | flops 2949636096 | bytes 9522048 | tf_op jit(solution)/shard_map/dot_general | solution.py:16
  264.5 5.6 %convolution_convert_fusion = bf16[3072,768]{1,0:T(8,128)(2,1)} fusion(bf16[624,3072]{1,0:T(8,128)(2,1)S(1)} %copy-done.110, bf16[624,768]{1,0:T(8,128)(2,1)S(1)} %copy-done.55), kind=kOutput, calls=%fused_computation.13 | convolution fusion | flops 2946760704 | bytes 9510912 | tf_op jit(solution)/shard_map/dot_general | solution.py:16
  270.1 3.6 add_convert_fusion.11
  279.2 5.5 %convolution_convert_fusion.2 = bf16[768,2304]{1,0:T(8,128)(2,1)S(1)} fusion(bf16[624,768]{1,0:T(8,128)(2,1)S(1)} %bitcast.203, bf16[624,2304]{0,1:T(8,128)(2,1)} %bitcast.197), kind=kOutput, calls=%fused_computation.15 | convolution fusion | flops 2210070528 | bytes 7372800 | tf_op jit(solution)/shard_map/dot_general | solution.py:16
  293.3 2.5 collective-permute-done.40
  304.4 2.2 copy.205
  310.7 3.4 collective-permute-start.50
  314.7 2.4 collective-permute-done.50
  331.4 4.9 collective-permute-done.43
  345.7 6.1 %collective-permute-done.45 = f32[96,768]{1,0:T(8,128)S(1)} collective-permute-done((f32[96,768]{1,0:T(8,128)S(1)}, f32[96,768]{1,0:T(8,128)S(1)}, u32[]{:S(2)}, u32[]{:S(2)}) %collective-permute-start.45) | collective-permute-done | bytes 294944 | tf_op jit(solution)/shard_map/ppermute | solution.py:48
  352.5 5.1 collective-permute-done.60
  360.4 3.7 collective-permute-done.61
  364.8 3.9 collective-permute-done.62
  370.1 3.7 collective-permute-done.63
  374.9 2.5 fusion.101
  381.8 2.5 collective-permute-start.65
  393.0 6.1 %collective-permute-done.52 = bf16[768,576]{0,1:T(8,128)(2,1)} collective-permute-done((bf16[768,576]{0,1:T(8,128)(2,1)}, bf16[768,576]{0,1:T(8,128)(2,1)}, u32[]{:S(2)}, u32[]{:S(2)}) %collective-permute-start.52) | collective-permute-done | bytes 884768 | tf_op jit(solution)/shard_map/ppermute | solution.py:48
  406.4 5.3 %collective-permute-done.53 = bf16[384,576]{1,0:T(8,128)(2,1)S(1)} collective-permute-done((bf16[384,576]{1,0:T(8,128)(2,1)S(1)}, bf16[384,576]{1,0:T(8,128)(2,1)S(1)}, u32[]{:S(2)}, u32[]{:S(2)}) %collective-permute-start.53) | collective-permute-done | bytes 442400 | tf_op jit(solution)/shard_map/ppermute | solution.py:48
  416.1 3.3 collective-permute-done.54
  422.9 3.9 collective-permute-done.55
  427.7 5.2 collective-permute-done.56
  433.1 11.7 %collective-permute-done.68 = bf16[768,768]{1,0:T(8,128)(2,1)S(1)} collective-permute-done((bf16[768,768]{1,0:T(8,128)(2,1)S(1)}, bf16[768,768]{1,0:T(8,128)(2,1)S(1)}, u32[]{:S(2)}, u32[]{:S(2)}) %collective-permute-start.68) | collective-permute-done | bytes 1179680 | tf_op jit(solution)/shard_map/ppermute | solution.py:48
  447.6 15.0 %collective-permute-done.76 = bf16[768,768]{1,0:T(8,128)(2,1)S(1)} collective-permute-done((bf16[768,768]{1,0:T(8,128)(2,1)S(1)}, bf16[768,768]{1,0:T(8,128)(2,1)S(1)}, u32[]{:S(2)}, u32[]{:S(2)}) %collective-permute-start.76) | collective-permute-done | bytes 1179680 | tf_op jit(solution)/shard_map/ppermute | solution.py:48
  467.8 9.8 %collective-permute-done.77 = bf16[384,768]{1,0:T(8,128)(2,1)S(1)} collective-permute-done((bf16[384,768]{1,0:T(8,128)(2,1)S(1)}, bf16[384,768]{1,0:T(8,128)(2,1)S(1)}, u32[]{:S(2)}, u32[]{:S(2)}) %collective-permute-start.77) | collective-permute-done | bytes 589856 | tf_op jit(solution)/shard_map/ppermute | solution.py:48
  481.0 6.7 %collective-permute-done.78 = bf16[192,768]{1,0:T(8,128)(2,1)S(1)} collective-permute-done((bf16[192,768]{1,0:T(8,128)(2,1)S(1)}, bf16[192,768]{1,0:T(8,128)(2,1)S(1)}, u32[]{:S(2)}, u32[]{:S(2)}) %collective-permute-start.78) | collective-permute-done | bytes 294944 | tf_op jit(solution)/shard_map/ppermute | solution.py:48
  491.0 4.1 collective-permute-done.79
  495.4 2.8 collective-permute-done.72
  514.1 3.6 collective-permute-done.74
  520.5 3.4 collective-permute-done.82
  (597 shorter events, 209.5 us)
Async XLA Ops:
  2.3 28.3 %collective-permute-start.3 = (bf16[12,192]{1,0:T(8,128)(2,1)S(1)}, bf16[12,192]{1,0:T(8,128)(2,1)S(1)}, u32[]{:S(2)}, u32[]{:S(2)}) collective-permute-start(bf16[12,192]{1,0:T(8,128)(2,1)S(1)} %bitcast.231), channel_id=1, source_target_pairs={{0,3},{1,2},{2,1},{3,0},{4,7},{5,6},{6,5},{7,4},{8,11},{9,10},{10,... | collective-permute-start | bytes 13832 | tf_op jit(solution)/shard_map/ppermute | solution.py:48
  4.8 26.5 %collective-permute-start.4 = (bf16[12,192]{1,0:T(8,128)(2,1)S(1)}, bf16[12,192]{1,0:T(8,128)(2,1)}, u32[]{:S(2)}, u32[]{:S(2)}) collective-permute-start(bf16[12,192]{1,0:T(8,128)(2,1)S(1)} %bitcast.232), channel_id=1, source_target_pairs={{0,2},{1,3},{2,0},{3,1},{4,6},{5,7},{6,4},{7,5},{8,10},{9,11},{10,... | collective-permute-start | bytes 13832 | tf_op jit(solution)/shard_map/ppermute | solution.py:48
  5.4 20.6 %collective-permute-start.21 = (f32[192]{0:T(256)}, f32[192]{0:T(256)}, u32[]{:S(2)}, u32[]{:S(2)}) collective-permute-start(f32[192]{0:T(256)} %param.43), channel_id=1, source_target_pairs={{0,2},{1,3},{2,0},{3,1},{4,6},{5,7},{6,4},{7,5},{8,10},{9,11},{10,... | collective-permute-start | bytes 2312 | tf_op jit(solution)/shard_map/ppermute | solution.py:48
  6.8 19.6 %collective-permute-start.23 = (f32[192]{0:T(256)}, f32[192]{0:T(256)}, u32[]{:S(2)}, u32[]{:S(2)}) collective-permute-start(f32[192]{0:T(256)} %param.43), channel_id=1, source_target_pairs={{0,1},{1,0},{2,3},{3,2},{4,5},{5,4},{6,7},{7,6},{8,9},{9,8},{10,11... | collective-permute-start | bytes 2312 | tf_op jit(solution)/shard_map/ppermute | solution.py:48
  6.9 19.8 %collective-permute-start.27 = (f32[192]{0:T(256)}, f32[192]{0:T(256)}, u32[]{:S(2)}, u32[]{:S(2)}) collective-permute-start(f32[192]{0:T(256)} %param.49), channel_id=1, source_target_pairs={{0,2},{1,3},{2,0},{3,1},{4,6},{5,7},{6,4},{7,5},{8,10},{9,11},{10,... | collective-permute-start | bytes 2312 | tf_op jit(solution)/shard_map/ppermute | solution.py:48
  28.4 10.1 %collective-permute-start.16 = (f32[2,192]{1,0:T(2,128)S(1)}, f32[2,192]{1,0:T(2,128)S(1)}, u32[]{:S(2)}, u32[]{:S(2)}) collective-permute-start(f32[2,192]{1,0:T(2,128)S(1)} %copy-done.101), channel_id=1, source_target_pairs={{0,2},{1,3},{2,0},{3,1},{4,6},{5,7},{6,4},{7,5},{8,10},{9,11},{10,... | collective-permute-start | bytes 4616 | tf_op jit(solution)/shard_map/ppermute | solution.py:48
  30.0 10.3 %collective-permute-start.15 = (f32[2,192]{1,0:T(2,128)S(1)}, f32[2,192]{1,0:T(2,128)S(1)}, u32[]{:S(2)}, u32[]{:S(2)}) collective-permute-start(f32[2,192]{1,0:T(2,128)S(1)} %copy-done.101), channel_id=1, source_target_pairs={{0,1},{1,0},{2,3},{3,2},{4,5},{5,4},{6,7},{7,6},{8,9},{9,8},{10,11... | collective-permute-start | bytes 4616 | tf_op jit(solution)/shard_map/ppermute | solution.py:48
  30.7 11.2 %collective-permute-start.25 = (f32[768]{0:T(1024)S(1)}, f32[768]{0:T(1024)S(1)}, u32[]{:S(2)}, u32[]{:S(2)}) collective-permute-start(f32[768]{0:T(1024)S(1)} %copy-done.94), channel_id=1, source_target_pairs={{0,2},{1,3},{2,0},{3,1},{4,6},{5,7},{6,4},{7,5},{8,10},{9,11},{10,... | collective-permute-start | bytes 9224 | tf_op jit(solution)/shard_map/ppermute | solution.py:48
  31.3 22.0 %collective-permute-start.24 = (f32[768]{0:T(1024)S(1)}, f32[768]{0:T(1024)S(1)}, u32[]{:S(2)}, u32[]{:S(2)}) collective-permute-start(f32[768]{0:T(1024)S(1)} %copy-done.94), channel_id=1, source_target_pairs={{0,1},{1,0},{2,3},{3,2},{4,5},{5,4},{6,7},{7,6},{8,9},{9,8},{10,11... | collective-permute-start | bytes 9224 | tf_op jit(solution)/shard_map/ppermute | solution.py:48
  38.5 20.8 %collective-permute-start.33 = (bf16[3,197,192]{2,1,0:T(8,128)(2,1)}, bf16[3,197,192]{2,1,0:T(8,128)(2,1)}, u32[]{:S(2)}, u32[]{:S(2)}) collective-permute-start(bf16[3,197,192]{2,1,0:T(8,128)(2,1)} %copy.230), channel_id=1, source_target_pairs={{0,3},{1,2},{2,1},{3,0},{4,7},{5,6},{6,5},{7,4},{8,11},{9,10},{10,... | collective-permute-start | bytes 680840 | tf_op jit(solution)/shard_map/ppermute | solution.py:48
  40.3 19.8 %collective-permute-start.34 = (bf16[3,197,192]{2,1,0:T(8,128)(2,1)}, bf16[3,197,192]{2,1,0:T(8,128)(2,1)}, u32[]{:S(2)}, u32[]{:S(2)}) collective-permute-start(bf16[3,197,192]{2,1,0:T(8,128)(2,1)} %copy.231), channel_id=1, source_target_pairs={{0,2},{1,3},{2,0},{3,1},{4,6},{5,7},{6,4},{7,5},{8,10},{9,11},{10,... | collective-permute-start | bytes 680840 | tf_op jit(solution)/shard_map/ppermute | solution.py:48
  41.9 12.3 %collective-permute-start.26 = (f32[768]{0:T(1024)S(1)}, f32[768]{0:T(1024)S(1)}, u32[]{:S(2)}, u32[]{:S(2)}) collective-permute-start(f32[768]{0:T(1024)S(1)} %collective-permute-done.25), channel_id=1, source_target_pairs={{0,1},{1,0},{2,3},{3,2},{4,5},{5,4},{6,7},{7,6},{8,9},{9,8},{10,11... | collective-permute-start | bytes 9224 | tf_op jit(solution)/shard_map/ppermute | solution.py:48
  42.1 6.9 %collective-permute-start.8 = (bf16[48,768]{1,0:T(8,128)(2,1)S(1)}, bf16[48,768]{1,0:T(8,128)(2,1)S(1)}, u32[]{:S(2)}, u32[]{:S(2)}) collective-permute-start(bf16[48,768]{1,0:T(8,128)(2,1)S(1)} %pad_maximum_fusion.32), channel_id=1, source_target_pairs={{0,16},{4,20},{8,24},{12,28},{16,0},{20,4},{24,8},{28,12},{1,17},{... | collective-permute-start | bytes 221192 | tf_op jit(solution)/shard_map/ppermute | solution.py:48
  53.3 8.2 %collective-permute-start.35 = (bf16[3,197,192]{2,1,0:T(8,128)(2,1)}, bf16[3,197,192]{2,1,0:T(8,128)(2,1)S(1)}, u32[]{:S(2)}, u32[]{:S(2)}) collective-permute-start(bf16[3,197,192]{2,1,0:T(8,128)(2,1)} %copy.232), channel_id=1, source_target_pairs={{0,1},{1,0},{2,3},{3,2},{4,5},{5,4},{6,7},{7,6},{8,9},{9,8},{10,11... | collective-permute-start | bytes 680840 | tf_op jit(solution)/shard_map/ppermute | solution.py:48
  57.8 37.0 %collective-permute-start.13 = (bf16[768,576]{0,1:T(8,128)(2,1)}, bf16[768,576]{0,1:T(8,128)(2,1)}, u32[]{:S(2)}, u32[]{:S(2)}) collective-permute-start(bf16[768,576]{0,1:T(8,128)(2,1)} %bitcast.204), channel_id=1, source_target_pairs={{0,2},{1,3},{2,0},{3,1},{4,6},{5,7},{6,4},{7,5},{8,10},{9,11},{10,... | collective-permute-start | bytes 2654216 | tf_op jit(solution)/shard_map/ppermute | solution.py:48
  59.2 42.7 %collective-permute-start.12 = (bf16[768,576]{0,1:T(8,128)(2,1)}, bf16[768,576]{0,1:T(8,128)(2,1)}, u32[]{:S(2)}, u32[]{:S(2)}) collective-permute-start(bf16[768,576]{0,1:T(8,128)(2,1)} %bitcast.205), channel_id=1, source_target_pairs={{0,1},{1,0},{2,3},{3,2},{4,5},{5,4},{6,7},{7,6},{8,9},{9,8},{10,11... | collective-permute-start | bytes 2654216 | tf_op jit(solution)/shard_map/ppermute | solution.py:48
  59.3 26.9 %collective-permute-start = (bf16[3,197,192]{2,1,0:T(8,128)(2,1)}, bf16[3,197,192]{2,1,0:T(8,128)(2,1)S(1)}, u32[]{:S(2)}, u32[]{:S(2)}) collective-permute-start(bf16[3,197,192]{2,1,0:T(8,128)(2,1)} %copy.225), channel_id=1, source_target_pairs={{0,3},{1,2},{2,1},{3,0},{4,7},{5,6},{6,5},{7,4},{8,11},{9,10},{10,... | collective-permute-start | bytes 680840 | tf_op jit(solution)/shard_map/ppermute | solution.py:48
  60.1 33.5 %collective-permute-start.1 = (bf16[3,197,192]{2,1,0:T(8,128)(2,1)}, bf16[3,197,192]{2,1,0:T(8,128)(2,1)S(1)}, u32[]{:S(2)}, u32[]{:S(2)}) collective-permute-start(bf16[3,197,192]{2,1,0:T(8,128)(2,1)} %copy.226), channel_id=1, source_target_pairs={{0,2},{1,3},{2,0},{3,1},{4,6},{5,7},{6,4},{7,5},{8,10},{9,11},{10,... | collective-permute-start | bytes 680840 | tf_op jit(solution)/shard_map/ppermute | solution.py:48
  61.5 32.1 %collective-permute-start.2 = (bf16[3,197,192]{2,1,0:T(8,128)(2,1)}, bf16[3,197,192]{2,1,0:T(8,128)(2,1)S(1)}, u32[]{:S(2)}, u32[]{:S(2)}) collective-permute-start(bf16[3,197,192]{2,1,0:T(8,128)(2,1)} %copy.227), channel_id=1, source_target_pairs={{0,1},{1,0},{2,3},{3,2},{4,5},{5,4},{6,7},{7,6},{8,9},{9,8},{10,11... | collective-permute-start | bytes 680840 | tf_op jit(solution)/shard_map/ppermute | solution.py:48
  86.2 62.5 %collective-permute-start.19 = (bf16[1728,768]{1,0:T(8,128)(2,1)}, bf16[1728,768]{1,0:T(8,128)(2,1)}, u32[]{:S(2)}, u32[]{:S(2)}) collective-permute-start(bf16[1728,768]{1,0:T(8,128)(2,1)} %constant_dynamic-update-slice_fusion), channel_id=1, source_target_pairs={{0,2},{1,3},{2,0},{3,1},{4,6},{5,7},{6,4},{7,5},{8,10},{9,11},{10,... | collective-permute-start | bytes 7962632 | tf_op jit(solution)/shard_map/ppermute | solution.py:48
  93.6 69.9 %collective-permute-start.18 = (bf16[1728,768]{1,0:T(8,128)(2,1)}, bf16[1728,768]{1,0:T(8,128)(2,1)}, u32[]{:S(2)}, u32[]{:S(2)}) collective-permute-start(bf16[1728,768]{1,0:T(8,128)(2,1)} %constant_dynamic-update-slice_fusion), channel_id=1, source_target_pairs={{0,1},{1,0},{2,3},{3,2},{4,5},{5,4},{6,7},{7,6},{8,9},{9,8},{10,11... | collective-permute-start | bytes 7962632 | tf_op jit(solution)/shard_map/ppermute | solution.py:48
  94.8 7.1 %collective-permute-start.14 = (bf16[768,576]{0,1:T(8,128)(2,1)}, bf16[768,576]{0,1:T(8,128)(2,1)}, u32[]{:S(2)}, u32[]{:S(2)}) collective-permute-start(bf16[768,576]{0,1:T(8,128)(2,1)} %collective-permute-done.13), channel_id=1, source_target_pairs={{0,1},{1,0},{2,3},{3,2},{4,5},{5,4},{6,7},{7,6},{8,9},{9,8},{10,11... | collective-permute-start | bytes 2654216 | tf_op jit(solution)/shard_map/ppermute | solution.py:48
  148.7 19.8 %collective-permute-start.20 = (bf16[1728,768]{1,0:T(8,128)(2,1)}, bf16[1728,768]{1,0:T(8,128)(2,1)}, u32[]{:S(2)}, u32[]{:S(2)}) collective-permute-start(bf16[1728,768]{1,0:T(8,128)(2,1)} %collective-permute-done.19), channel_id=1, source_target_pairs={{0,1},{1,0},{2,3},{3,2},{4,5},{5,4},{6,7},{7,6},{8,9},{9,8},{10,11... | collective-permute-start | bytes 7962632 | tf_op jit(solution)/shard_map/ppermute | solution.py:48
  275.1 46.3 %collective-permute-start.30 = (bf16[3,197,192]{2,1,0:T(8,128)(2,1)}, bf16[3,197,192]{2,1,0:T(8,128)(2,1)}, u32[]{:S(2)}, u32[]{:S(2)}) collective-permute-start(bf16[3,197,192]{2,1,0:T(8,128)(2,1)} %get-tuple-element.209), channel_id=1, source_target_pairs={{0,3},{1,2},{2,1},{3,0},{4,7},{5,6},{6,5},{7,4},{8,11},{9,10},{10,... | collective-permute-start | bytes 680840 | tf_op jit(solution)/shard_map/ppermute | solution.py:48
  276.5 44.8 %collective-permute-start.31 = (bf16[3,197,192]{2,1,0:T(8,128)(2,1)}, bf16[3,197,192]{2,1,0:T(8,128)(2,1)}, u32[]{:S(2)}, u32[]{:S(2)}) collective-permute-start(bf16[3,197,192]{2,1,0:T(8,128)(2,1)} %get-tuple-element.210), channel_id=1, source_target_pairs={{0,2},{1,3},{2,0},{3,1},{4,6},{5,7},{6,4},{7,5},{8,10},{9,11},{10,... | collective-permute-start | bytes 680840 | tf_op jit(solution)/shard_map/ppermute | solution.py:48
  277.2 44.6 %collective-permute-start.32 = (bf16[3,197,192]{2,1,0:T(8,128)(2,1)}, bf16[3,197,192]{2,1,0:T(8,128)(2,1)}, u32[]{:S(2)}, u32[]{:S(2)}) collective-permute-start(bf16[3,197,192]{2,1,0:T(8,128)(2,1)} %get-tuple-element.208), channel_id=1, source_target_pairs={{0,1},{1,0},{2,3},{3,2},{4,5},{5,4},{6,7},{7,6},{8,9},{9,8},{10,11... | collective-permute-start | bytes 680840 | tf_op jit(solution)/shard_map/ppermute | solution.py:48
  278.6 13.3 %collective-permute-start.39 = (f32[3,768]{1,0:T(4,128)S(1)}, f32[3,768]{1,0:T(4,128)S(1)}, u32[]{:S(2)}, u32[]{:S(2)}) collective-permute-start(f32[3,768]{1,0:T(4,128)S(1)} %bitcast.236), channel_id=1, source_target_pairs={{0,1},{1,0},{2,3},{3,2},{4,5},{5,4},{6,7},{7,6},{8,9},{9,8},{10,11... | collective-permute-start | bytes 27656 | tf_op jit(solution)/shard_map/ppermute | solution.py:48
  279.2 18.2 %collective-permute-start.46 = (f32[72,128]{1,0:T(8,128)S(1)}, f32[72,128]{1,0:T(8,128)S(1)}, u32[]{:S(2)}, u32[]{:S(2)}) collective-permute-start(f32[72,128]{1,0:T(8,128)S(1)} %bitcast.216), channel_id=1, source_target_pairs={{0,1},{1,0},{2,3},{3,2},{4,5},{5,4},{6,7},{7,6},{8,9},{9,8},{10,11... | collective-permute-start | bytes 110600 | tf_op jit(solution)/shard_map/ppermute | solution.py:48
  306.6 18.4 %collective-permute-start.36 = (bf16[3,197,192]{2,1,0:T(8,128)(2,1)}, bf16[3,197,192]{2,1,0:T(8,128)(2,1)}, u32[]{:S(2)}, u32[]{:S(2)}) collective-permute-start(bf16[3,197,192]{2,1,0:T(8,128)(2,1)} %get-tuple-element.204), channel_id=1, source_target_pairs={{0,3},{1,2},{2,1},{3,0},{4,7},{5,6},{6,5},{7,4},{8,11},{9,10},{10,... | collective-permute-start | bytes 680840 | tf_op jit(solution)/shard_map/ppermute | solution.py:48
  310.7 6.5 %collective-permute-start.50 = (f32[72,128]{1,0:T(8,128)S(1)}, f32[72,128]{1,0:T(8,128)S(1)}, u32[]{:S(2)}, u32[]{:S(2)}) collective-permute-start(f32[72,128]{1,0:T(8,128)S(1)} %add.403), channel_id=1, source_target_pairs={{0,16},{4,20},{8,24},{12,28},{16,0},{20,4},{24,8},{28,12},{1,17},{... | collective-permute-start | bytes 110600 | tf_op jit(solution)/shard_map/ppermute | solution.py:48
  317.2 9.6 %collective-permute-start.37 = (bf16[3,197,192]{2,1,0:T(8,128)(2,1)}, bf16[3,197,192]{2,1,0:T(8,128)(2,1)}, u32[]{:S(2)}, u32[]{:S(2)}) collective-permute-start(bf16[3,197,192]{2,1,0:T(8,128)(2,1)} %get-tuple-element.205), channel_id=1, source_target_pairs={{0,2},{1,3},{2,0},{3,1},{4,6},{5,7},{6,4},{7,5},{8,10},{9,11},{10,... | collective-permute-start | bytes 680840 | tf_op jit(solution)/shard_map/ppermute | solution.py:48
  321.3 5.4 %collective-permute-start.38 = (bf16[3,197,192]{2,1,0:T(8,128)(2,1)}, bf16[3,197,192]{2,1,0:T(8,128)(2,1)}, u32[]{:S(2)}, u32[]{:S(2)}) collective-permute-start(bf16[3,197,192]{2,1,0:T(8,128)(2,1)} %get-tuple-element.203), channel_id=1, source_target_pairs={{0,1},{1,0},{2,3},{3,2},{4,5},{5,4},{6,7},{7,6},{8,9},{9,8},{10,11... | collective-permute-start | bytes 680840 | tf_op jit(solution)/shard_map/ppermute | solution.py:48
  321.4 53.6 %collective-permute-start.51 = (bf16[1536,576]{0,1:T(8,128)(2,1)}, bf16[1536,576]{0,1:T(8,128)(2,1)}, u32[]{:S(2)}, u32[]{:S(2)}) collective-permute-start(bf16[1536,576]{0,1:T(8,128)(2,1)} %copy.205), channel_id=1, source_target_pairs={{0,1},{1,0},{2,3},{3,2},{4,5},{5,4},{6,7},{7,6},{8,9},{9,8},{10,11... | collective-permute-start | bytes 5308424 | tf_op jit(solution)/shard_map/ppermute | solution.py:48
  321.9 21.3 %collective-permute-start.59 = (bf16[384,768]{1,0:T(8,128)(2,1)}, bf16[384,768]{1,0:T(8,128)(2,1)}, u32[]{:S(2)}, u32[]{:S(2)}) collective-permute-start(bf16[384,768]{1,0:T(8,128)(2,1)} %pad_maximum_fusion.14), channel_id=1, source_target_pairs={{0,1},{1,0},{2,3},{3,2},{4,5},{5,4},{6,7},{7,6},{8,9},{9,8},{10,11... | collective-permute-start | bytes 1769480 | tf_op jit(solution)/shard_map/ppermute | solution.py:48
  325.0 88.8 %collective-permute-start.67 = (bf16[1536,768]{1,0:T(8,128)(2,1)}, bf16[1536,768]{1,0:T(8,128)(2,1)}, u32[]{:S(2)}, u32[]{:S(2)}) collective-permute-start(bf16[1536,768]{1,0:T(8,128)(2,1)} %pad_maximum_fusion.3), channel_id=1, source_target_pairs={{0,1},{1,0},{2,3},{3,2},{4,5},{5,4},{6,7},{7,6},{8,9},{9,8},{10,11... | collective-permute-start | bytes 7077896 | tf_op jit(solution)/shard_map/ppermute | solution.py:48
  326.7 94.1 %collective-permute-start.75 = (bf16[1536,768]{1,0:T(8,128)(2,1)}, bf16[1536,768]{1,0:T(8,128)(2,1)}, u32[]{:S(2)}, u32[]{:S(2)}) collective-permute-start(bf16[1536,768]{1,0:T(8,128)(2,1)} %pad_maximum_fusion.4), channel_id=1, source_target_pairs={{0,1},{1,0},{2,3},{3,2},{4,5},{5,4},{6,7},{7,6},{8,9},{9,8},{10,11... | collective-permute-start | bytes 7077896 | tf_op jit(solution)/shard_map/ppermute | solution.py:48
  326.8 9.5 %collective-permute-start.43 = (f32[48,768]{1,0:T(8,128)}, f32[48,768]{1,0:T(8,128)S(1)}, u32[]{:S(2)}, u32[]{:S(2)}) collective-permute-start(f32[48,768]{1,0:T(8,128)} %pad_maximum_fusion.27), channel_id=1, source_target_pairs={{0,16},{4,20},{8,24},{12,28},{16,0},{20,4},{24,8},{28,12},{1,17},{... | collective-permute-start | bytes 442376 | tf_op jit(solution)/shard_map/ppermute | solution.py:48
  341.9 9.9 %collective-permute-start.45 = (f32[96,768]{1,0:T(8,128)S(1)}, f32[96,768]{1,0:T(8,128)S(1)}, u32[]{:S(2)}, u32[]{:S(2)}) collective-permute-start(f32[96,768]{1,0:T(8,128)S(1)} %add.395), channel_id=1, source_target_pairs={{0,2},{1,3},{2,0},{3,1},{4,6},{5,7},{6,4},{7,5},{8,10},{9,11},{10,... | collective-permute-start | bytes 884744 | tf_op jit(solution)/shard_map/ppermute | solution.py:48
  344.2 13.4 %collective-permute-start.60 = (bf16[192,768]{1,0:T(8,128)(2,1)S(1)}, bf16[192,768]{1,0:T(8,128)(2,1)S(1)}, u32[]{:S(2)}, u32[]{:S(2)}) collective-permute-start(bf16[192,768]{1,0:T(8,128)(2,1)S(1)} %add_convert_fusion.19), channel_id=1, source_target_pairs={{0,2},{1,3},{2,0},{3,1},{4,6},{5,7},{6,4},{7,5},{8,10},{9,11},{10,... | collective-permute-start | bytes 884744 | tf_op jit(solution)/shard_map/ppermute | solution.py:48
  358.7 5.5 %collective-permute-start.61 = (bf16[96,768]{1,0:T(8,128)(2,1)S(1)}, bf16[96,768]{1,0:T(8,128)(2,1)S(1)}, u32[]{:S(2)}, u32[]{:S(2)}) collective-permute-start(bf16[96,768]{1,0:T(8,128)(2,1)S(1)} %broadcast_select_fusion.74), channel_id=1, source_target_pairs={{0,4},{4,0},{8,12},{12,8},{16,20},{20,16},{24,28},{28,24},{1,5},{5... | collective-permute-start | bytes 442376 | tf_op jit(solution)/shard_map/ppermute | solution.py:48
  373.8 7.3 %collective-permute-start.64 = (bf16[24,768]{1,0:T(8,128)(2,1)S(1)}, bf16[24,768]{1,0:T(8,128)(2,1)S(1)}, u32[]{:S(2)}, u32[]{:S(2)}) collective-permute-start(bf16[24,768]{1,0:T(8,128)(2,1)S(1)} %add_convert_fusion.29), channel_id=1, source_target_pairs={{0,16},{4,20},{8,24},{12,28},{16,0},{20,4},{24,8},{28,12},{1,17},{... | collective-permute-start | bytes 110600 | tf_op jit(solution)/shard_map/ppermute | solution.py:48
  380.8 18.4 %collective-permute-start.52 = (bf16[768,576]{0,1:T(8,128)(2,1)}, bf16[768,576]{0,1:T(8,128)(2,1)}, u32[]{:S(2)}, u32[]{:S(2)}) collective-permute-start(bf16[768,576]{0,1:T(8,128)(2,1)} %copy.208), channel_id=1, source_target_pairs={{0,2},{1,3},{2,0},{3,1},{4,6},{5,7},{6,4},{7,5},{8,10},{9,11},{10,... | collective-permute-start | bytes 2654216 | tf_op jit(solution)/shard_map/ppermute | solution.py:48
  381.8 8.3 %collective-permute-start.65 = (bf16[48,768]{1,0:T(8,128)(2,1)}, bf16[48,768]{1,0:T(8,128)(2,1)}, u32[]{:S(2)}, u32[]{:S(2)}) collective-permute-start(bf16[48,768]{1,0:T(8,128)(2,1)} %pad_maximum_fusion.34), channel_id=1, source_target_pairs={{0,8},{4,12},{8,0},{12,4},{16,24},{20,28},{24,16},{28,20},{1,9},{5... | collective-permute-start | bytes 221192 | tf_op jit(solution)/shard_map/ppermute | solution.py:48
  391.7 13.7 %collective-permute-start.66 = (bf16[96,768]{1,0:T(8,128)(2,1)}, bf16[96,768]{1,0:T(8,128)(2,1)}, u32[]{:S(2)}, u32[]{:S(2)}) collective-permute-start(bf16[96,768]{1,0:T(8,128)(2,1)} %pad_maximum_fusion.29), channel_id=1, source_target_pairs={{0,4},{4,0},{8,12},{12,8},{16,20},{20,16},{24,28},{28,24},{1,5},{5... | collective-permute-start | bytes 442376 | tf_op jit(solution)/shard_map/ppermute | solution.py:48
  402.8 8.9 %collective-permute-start.53 = (bf16[384,576]{1,0:T(8,128)(2,1)S(1)}, bf16[384,576]{1,0:T(8,128)(2,1)S(1)}, u32[]{:S(2)}, u32[]{:S(2)}) collective-permute-start(bf16[384,576]{1,0:T(8,128)(2,1)S(1)} %broadcast_select_fusion.8), channel_id=1, source_target_pairs={{0,4},{4,0},{8,12},{12,8},{16,20},{20,16},{24,28},{28,24},{1,5},{5... | collective-permute-start | bytes 1327112 | tf_op jit(solution)/shard_map/ppermute | solution.py:48
  411.9 7.5 %collective-permute-start.54 = (bf16[192,576]{1,0:T(8,128)(2,1)S(1)}, bf16[192,576]{1,0:T(8,128)(2,1)S(1)}, u32[]{:S(2)}, u32[]{:S(2)}) collective-permute-start(bf16[192,576]{1,0:T(8,128)(2,1)S(1)} %broadcast_select_fusion.65), channel_id=1, source_target_pairs={{0,8},{4,12},{8,0},{12,4},{16,24},{20,28},{24,16},{28,20},{1,9},{5... | collective-permute-start | bytes 663560 | tf_op jit(solution)/shard_map/ppermute | solution.py:48
  415.7 29.0 %collective-permute-start.68 = (bf16[768,768]{1,0:T(8,128)(2,1)S(1)}, bf16[768,768]{1,0:T(8,128)(2,1)S(1)}, u32[]{:S(2)}, u32[]{:S(2)}) collective-permute-start(bf16[768,768]{1,0:T(8,128)(2,1)S(1)} %add_convert_fusion.6), channel_id=1, source_target_pairs={{0,2},{1,3},{2,0},{3,1},{4,6},{5,7},{6,4},{7,5},{8,10},{9,11},{10,... | collective-permute-start | bytes 3538952 | tf_op jit(solution)/shard_map/ppermute | solution.py:48
  419.6 7.2 %collective-permute-start.55 = (bf16[96,576]{1,0:T(8,128)(2,1)S(1)}, bf16[96,576]{1,0:T(8,128)(2,1)S(1)}, u32[]{:S(2)}, u32[]{:S(2)}) collective-permute-start(bf16[96,576]{1,0:T(8,128)(2,1)S(1)} %broadcast_select_fusion.77), channel_id=1, source_target_pairs={{0,16},{4,20},{8,24},{12,28},{16,0},{20,4},{24,8},{28,12},{1,17},{... | collective-permute-start | bytes 331784 | tf_op jit(solution)/shard_map/ppermute | solution.py:48
  422.5 40.1 %collective-permute-start.76 = (bf16[768,768]{1,0:T(8,128)(2,1)S(1)}, bf16[768,768]{1,0:T(8,128)(2,1)S(1)}, u32[]{:S(2)}, u32[]{:S(2)}) collective-permute-start(bf16[768,768]{1,0:T(8,128)(2,1)S(1)} %add_convert_fusion.3), channel_id=1, source_target_pairs={{0,2},{1,3},{2,0},{3,1},{4,6},{5,7},{6,4},{7,5},{8,10},{9,11},{10,... | collective-permute-start | bytes 3538952 | tf_op jit(solution)/shard_map/ppermute | solution.py:48
  426.8 6.1 %collective-permute-start.56 = (bf16[96,576]{1,0:T(8,128)(2,1)S(1)}, bf16[96,576]{1,0:T(8,128)(2,1)S(1)}, u32[]{:S(2)}, u32[]{:S(2)}) collective-permute-start(bf16[96,576]{1,0:T(8,128)(2,1)S(1)} %add_convert_fusion.27), channel_id=1, source_target_pairs={{0,16},{4,20},{8,24},{12,28},{16,0},{20,4},{24,8},{28,12},{1,17},{... | collective-permute-start | bytes 331784 | tf_op jit(solution)/shard_map/ppermute | solution.py:48
  433.0 32.1 %collective-permute-start.57 = (bf16[192,576]{1,0:T(8,128)(2,1)S(1)}, bf16[192,576]{1,0:T(8,128)(2,1)S(1)}, u32[]{:S(2)}, u32[]{:S(2)}) collective-permute-start(bf16[192,576]{1,0:T(8,128)(2,1)S(1)} %pad_maximum_fusion.21), channel_id=1, source_target_pairs={{0,8},{4,12},{8,0},{12,4},{16,24},{20,28},{24,16},{28,20},{1,9},{5... | collective-permute-start | bytes 663560 | tf_op jit(solution)/shard_map/ppermute | solution.py:48
  446.9 19.8 %collective-permute-start.69 = (bf16[384,768]{1,0:T(8,128)(2,1)S(1)}, bf16[384,768]{1,0:T(8,128)(2,1)S(1)}, u32[]{:S(2)}, u32[]{:S(2)}) collective-permute-start(bf16[384,768]{1,0:T(8,128)(2,1)S(1)} %broadcast_select_fusion.5), channel_id=1, source_target_pairs={{0,4},{4,0},{8,12},{12,8},{16,20},{20,16},{24,28},{28,24},{1,5},{5... | collective-permute-start | bytes 1769480 | tf_op jit(solution)/shard_map/ppermute | solution.py:48
  464.4 13.2 %collective-permute-start.77 = (bf16[384,768]{1,0:T(8,128)(2,1)S(1)}, bf16[384,768]{1,0:T(8,128)(2,1)S(1)}, u32[]{:S(2)}, u32[]{:S(2)}) collective-permute-start(bf16[384,768]{1,0:T(8,128)(2,1)S(1)} %broadcast_select_fusion.2), channel_id=1, source_target_pairs={{0,4},{4,0},{8,12},{12,8},{16,20},{20,16},{24,28},{28,24},{1,5},{5... | collective-permute-start | bytes 1769480 | tf_op jit(solution)/shard_map/ppermute | solution.py:48
  465.2 41.8 %collective-permute-start.58 = (bf16[384,576]{1,0:T(8,128)(2,1)S(1)}, bf16[384,576]{1,0:T(8,128)(2,1)S(1)}, u32[]{:S(2)}, u32[]{:S(2)}) collective-permute-start(bf16[384,576]{1,0:T(8,128)(2,1)S(1)} %pad_maximum_fusion.17), channel_id=1, source_target_pairs={{0,4},{4,0},{8,12},{12,8},{16,20},{20,16},{24,28},{28,24},{1,5},{5... | collective-permute-start | bytes 1327112 | tf_op jit(solution)/shard_map/ppermute | solution.py:48
  467.0 12.4 %collective-permute-start.70 = (bf16[192,768]{1,0:T(8,128)(2,1)S(1)}, bf16[192,768]{1,0:T(8,128)(2,1)S(1)}, u32[]{:S(2)}, u32[]{:S(2)}) collective-permute-start(bf16[192,768]{1,0:T(8,128)(2,1)S(1)} %broadcast_select_fusion.62), channel_id=1, source_target_pairs={{0,8},{4,12},{8,0},{12,4},{16,24},{20,28},{24,16},{28,20},{1,9},{5... | collective-permute-start | bytes 884744 | tf_op jit(solution)/shard_map/ppermute | solution.py:48
  477.9 9.9 %collective-permute-start.78 = (bf16[192,768]{1,0:T(8,128)(2,1)S(1)}, bf16[192,768]{1,0:T(8,128)(2,1)S(1)}, u32[]{:S(2)}, u32[]{:S(2)}) collective-permute-start(bf16[192,768]{1,0:T(8,128)(2,1)S(1)} %broadcast_select_fusion.59), channel_id=1, source_target_pairs={{0,8},{4,12},{8,0},{12,4},{16,24},{20,28},{24,16},{28,20},{1,9},{5... | collective-permute-start | bytes 884744 | tf_op jit(solution)/shard_map/ppermute | solution.py:48
  479.5 10.6 %collective-permute-start.71 = (bf16[96,768]{1,0:T(8,128)(2,1)S(1)}, bf16[96,768]{1,0:T(8,128)(2,1)S(1)}, u32[]{:S(2)}, u32[]{:S(2)}) collective-permute-start(bf16[96,768]{1,0:T(8,128)(2,1)S(1)} %broadcast_select_fusion.71), channel_id=1, source_target_pairs={{0,16},{4,20},{8,24},{12,28},{16,0},{20,4},{24,8},{28,12},{1,17},{... | collective-permute-start | bytes 442376 | tf_op jit(solution)/shard_map/ppermute | solution.py:48
  487.9 7.2 %collective-permute-start.79 = (bf16[96,768]{1,0:T(8,128)(2,1)S(1)}, bf16[96,768]{1,0:T(8,128)(2,1)S(1)}, u32[]{:S(2)}, u32[]{:S(2)}) collective-permute-start(bf16[96,768]{1,0:T(8,128)(2,1)S(1)} %broadcast_select_fusion.68), channel_id=1, source_target_pairs={{0,16},{4,20},{8,24},{12,28},{16,0},{20,4},{24,8},{28,12},{1,17},{... | collective-permute-start | bytes 442376 | tf_op jit(solution)/shard_map/ppermute | solution.py:48
  490.2 8.0 %collective-permute-start.72 = (bf16[96,768]{1,0:T(8,128)(2,1)S(1)}, bf16[96,768]{1,0:T(8,128)(2,1)S(1)}, u32[]{:S(2)}, u32[]{:S(2)}) collective-permute-start(bf16[96,768]{1,0:T(8,128)(2,1)S(1)} %add_convert_fusion.23), channel_id=1, source_target_pairs={{0,16},{4,20},{8,24},{12,28},{16,0},{20,4},{24,8},{28,12},{1,17},{... | collective-permute-start | bytes 442376 | tf_op jit(solution)/shard_map/ppermute | solution.py:48
  495.2 6.8 %collective-permute-start.80 = (bf16[96,768]{1,0:T(8,128)(2,1)S(1)}, bf16[96,768]{1,0:T(8,128)(2,1)S(1)}, u32[]{:S(2)}, u32[]{:S(2)}) collective-permute-start(bf16[96,768]{1,0:T(8,128)(2,1)S(1)} %add_convert_fusion.22), channel_id=1, source_target_pairs={{0,16},{4,20},{8,24},{12,28},{16,0},{20,4},{24,8},{28,12},{1,17},{... | collective-permute-start | bytes 442376 | tf_op jit(solution)/shard_map/ppermute | solution.py:48
  498.3 6.8 %collective-permute-start.73 = (bf16[192,768]{1,0:T(8,128)(2,1)S(1)}, bf16[192,768]{1,0:T(8,128)(2,1)S(1)}, u32[]{:S(2)}, u32[]{:S(2)}) collective-permute-start(bf16[192,768]{1,0:T(8,128)(2,1)S(1)} %pad_maximum_fusion.19), channel_id=1, source_target_pairs={{0,8},{4,12},{8,0},{12,4},{16,24},{20,28},{24,16},{28,20},{1,9},{5... | collective-permute-start | bytes 884744 | tf_op jit(solution)/shard_map/ppermute | solution.py:48
  502.7 7.0 %collective-permute-start.81 = (bf16[192,768]{1,0:T(8,128)(2,1)}, bf16[192,768]{1,0:T(8,128)(2,1)}, u32[]{:S(2)}, u32[]{:S(2)}) collective-permute-start(bf16[192,768]{1,0:T(8,128)(2,1)} %pad_maximum_fusion.20), channel_id=1, source_target_pairs={{0,8},{4,12},{8,0},{12,4},{16,24},{20,28},{24,16},{28,20},{1,9},{5... | collective-permute-start | bytes 884744 | tf_op jit(solution)/shard_map/ppermute | solution.py:48
  506.0 11.6 %collective-permute-start.74 = (bf16[384,768]{1,0:T(8,128)(2,1)}, bf16[384,768]{1,0:T(8,128)(2,1)}, u32[]{:S(2)}, u32[]{:S(2)}) collective-permute-start(bf16[384,768]{1,0:T(8,128)(2,1)} %pad_maximum_fusion.15), channel_id=1, source_target_pairs={{0,4},{4,0},{8,12},{12,8},{16,20},{20,16},{24,28},{28,24},{1,5},{5... | collective-permute-start | bytes 1769480 | tf_op jit(solution)/shard_map/ppermute | solution.py:48
  510.9 13.0 %collective-permute-start.82 = (bf16[384,768]{1,0:T(8,128)(2,1)S(1)}, bf16[384,768]{1,0:T(8,128)(2,1)S(1)}, u32[]{:S(2)}, u32[]{:S(2)}) collective-permute-start(bf16[384,768]{1,0:T(8,128)(2,1)S(1)} %pad_maximum_fusion.16), channel_id=1, source_target_pairs={{0,4},{4,0},{8,12},{12,8},{16,20},{20,16},{24,28},{28,24},{1,5},{5... | collective-permute-start | bytes 1769480 | tf_op jit(solution)/shard_map/ppermute | solution.py:48
  (136 other events, 812.2 us)
